TPU v7x, 768 devices: a whole 4x8x12 slice. The times are simulated.
768 devices in a mesh: section: 16 (over y_lo, x), expert: 48 (over z, y_hi, core).
Axes of the slice: x: 4, y: 8 (y_hi: 2, y_lo: 4; y = y_hi * 4 + y_lo), z: 12, core: 2. Of those that a mesh axis runs over, the one named last changes fastest.
Arguments:
- fwd_held: bfloat16 [16, 3072, 3584], P('section', 'expert'), may hold values from -6 to 6
- saved_preact: bfloat16 [16, 48, 2, 2, 6144], P('section', None, None, None, 'expert'), may hold values from -6 to 6
- grad_held: bfloat16 [16, 3072, 3584], P('section', 'expert'), may hold values from -6 to 6
- gate_weight: bfloat16 [16, 3584, 6144], P('section', None, 'expert'), may hold values from -0.09375 to 0.09375
- up_weight: bfloat16 [16, 3584, 6144], P('section', None, 'expert'), may hold values from -0.09375 to 0.09375
- down_weight: bfloat16 [16, 6144, 3584], P('section', 'expert'), may hold values from -0.125 to 0.125
- fwd_slots: int32 [16, 48, 3, 2], P('section', 'expert'), may hold values from 0 to 64, as said below
- fwd_gates: float32 [16, 48, 3, 2], P('section', 'expert'), may hold values from 0.2 to 1
- bwd_slots: int32 [16, 48, 3, 2], P('section', 'expert'), may hold values from 0 to 64, as said below
- bwd_gates: float32 [16, 48, 3, 2], P('section', 'expert'), may hold values from 0.2 to 1
Outputs:
- fwd_out: bfloat16 [16, 3072, 3584], P('section', 'expert')
- grad_out: bfloat16 [16, 3072, 3584], P('section', 'expert')
Inputs may be any that keep to these rules, and one draw needn't show every extreme that they name: `fwd_slots`: each entry names a token of the same device's block of 64 tokens, or 64 for an empty slot; the filled slots of one section, device and expert name distinct tokens. `bwd_slots`: each entry names a token of the same device's block of 64 tokens, or 64 for an empty slot; the filled slots of one section, device and expert name distinct tokens.
All inputs are finite; a program needn't handle non-finite values.
Results may differ from a plain program's by a relative error of at most 0.0023.
Values may be sent and summed in bfloat16 or wider, within the bound.
No kernel may reach another device: no remote copies, remote signals or barrier semaphores. Data moves between devices by JAX's collectives and lax.ppermute only.
A program may use at most 32 MiB of HBM per device.

v0:
```python
import jax
import jax.numpy as jnp
from jax import lax
from jax.sharding import PartitionSpec as P


def shifted(shard, axis, by):
    length = lax.axis_size(axis)
    return lax.ppermute(shard, axis, [(i, (i + by) % length) for i in range(length)])


def pick_rows(slots, block):
    count = block.shape[0]
    flat = slots.reshape(-1)
    onehot = flat[:, None] == jnp.arange(count, dtype=jnp.int32)[None, :]
    rows = jnp.dot(onehot.astype(jnp.bfloat16), block, preferred_element_type=jnp.float32).astype(
        jnp.bfloat16
    )
    return (onehot.astype(jnp.float32), rows)


def spread(rows, groups, split, width):
    sectioned = rows.reshape(groups, 1, -1, width)
    sectioned = jnp.broadcast_to(sectioned, (groups, split, sectioned.shape[2], width))
    return sectioned.reshape(groups * split, -1, width)


def settle(back, groups, split, onehot, gates, block):
    width = block.shape[1]
    summed = (
        back.astype(jnp.float32).reshape(groups, split, -1, width).sum(axis=1).reshape(-1, width)
    )
    weighted = onehot * gates.reshape(-1)[:, None]
    added = lax.dot_general(
        weighted, summed, (((0,), (0,)), ((), ())), precision=lax.Precision.HIGHEST
    )
    return (block.astype(jnp.float32) + added).astype(jnp.bfloat16)


def local(
    fwd_held,
    saved_preact,
    grad_held,
    gate_weight,
    up_weight,
    down_weight,
    fwd_slots,
    fwd_gates,
    bwd_slots,
    bwd_gates,
):
    width = fwd_held.shape[2]
    groups = fwd_slots.shape[2]
    split = lax.axis_size("expert") // groups
    w_gate = gate_weight[0]
    w_up = up_weight[0]
    w_down = down_weight[0]
    from_below = shifted(fwd_held, "section", 1)
    from_above = shifted(grad_held, "section", -1)
    inputs = from_below[0]
    incoming = from_above[0]
    fwd_hot, fwd_rows = pick_rows(fwd_slots[0, 0], inputs)
    fwd_send = spread(fwd_rows, groups, split, width)
    piece = lax.all_to_all(fwd_send, "expert", split_axis=0, concat_axis=0, tiled=True)
    lead = piece.shape[0]
    items = piece.shape[1]
    flat = piece.reshape(lead * items, width)
    pre_gate = jnp.dot(flat, w_gate, preferred_element_type=jnp.float32)
    pre_up = jnp.dot(flat, w_up, preferred_element_type=jnp.float32)
    hidden = (jax.nn.silu(pre_gate) * pre_up).astype(jnp.bfloat16)
    partial_value = jnp.dot(hidden, w_down, preferred_element_type=jnp.float32).astype(jnp.bfloat16)
    fwd_back = lax.all_to_all(
        partial_value.reshape(lead, items, width), "expert", split_axis=0, concat_axis=0, tiled=True
    )
    fwd_out = settle(fwd_back, groups, split, fwd_hot, fwd_gates[0, 0], inputs)
    bwd_hot, grad_rows = pick_rows(bwd_slots[0, 0], incoming)
    grad_send = spread(grad_rows, groups, split, width)
    arrived = lax.all_to_all(grad_send, "expert", split_axis=0, concat_axis=0, tiled=True)
    lead = arrived.shape[0]
    flat = arrived.reshape(-1, width)
    dh = lax.dot_general(flat, w_down, (((1,), (1,)), ((), ())), preferred_element_type=jnp.float32)
    hidden_width = w_down.shape[0]
    pre_a = saved_preact[0, :, :, 0, :].reshape(-1, hidden_width).astype(jnp.float32)
    pre_v = saved_preact[0, :, :, 1, :].reshape(-1, hidden_width).astype(jnp.float32)
    sig = jax.nn.sigmoid(pre_a)
    act = pre_a * sig
    slope = sig * (1.0 + pre_a * (1.0 - sig))
    d_both = jnp.concatenate([dh * pre_v * slope, dh * act], axis=1).astype(jnp.bfloat16)
    w_both = jnp.concatenate([w_gate, w_up], axis=1)
    partial_value = lax.dot_general(
        d_both, w_both, (((1,), (1,)), ((), ())), preferred_element_type=jnp.float32
    )
    partial_value = partial_value.astype(jnp.bfloat16).reshape(lead, -1, width)
    grad_back = lax.all_to_all(partial_value, "expert", split_axis=0, concat_axis=0, tiled=True)
    grad_out = settle(grad_back, groups, split, bwd_hot, bwd_gates[0, 0], incoming)
    return (fwd_out[None], grad_out[None])


def solution(mesh):
    in_specs = (
        P("section", "expert", None),
        P("section", None, None, None, "expert"),
        P("section", "expert", None),
        P("section", None, "expert"),
        P("section", None, "expert"),
        P("section", "expert", None),
        P("section", "expert", None, None),
        P("section", "expert", None, None),
        P("section", "expert", None, None),
        P("section", "expert", None, None),
    )
    out_specs = (P("section", "expert", None), P("section", "expert", None))
    return jax.shard_map(local, mesh=mesh, in_specs=in_specs, out_specs=out_specs, check_vma=False)
```

profile of v0, /device:TPU:1, one launch (start us, length us, event | category | flops | bytes accessed | tf_op | source)
XLA Modules:
  0.0 204.5 jit_solution(360323543413181824)
XLA Ops:
  0.6 8.4 %collective-permute-start.1 = (bf16[1,64,3584]{2,1,0:T(8,128)(2,1)}, bf16[1,64,3584]{2,1,0:T(8,128)(2,1)S(1)}, u32[]{:S(2)}, u32[]{:S(2)}) collective-permute-start(bf16[1,64,3584]{2,1,0:T(8,128)(2,1)} %param.12), channel_id=1, source_target_pairs={{0,720},{48,0},{96,48},{144,96},{192,144},{240,192},{288,240},{336... | collective-permute-start | bytes 1376264 | tf_op jit(solution)/shard_map/ppermute | solution.py:9
  9.0 0.8 copy.18
  9.9 5.3 %collective-permute-done.1 = bf16[1,64,3584]{2,1,0:T(8,128)(2,1)S(1)} collective-permute-done((bf16[1,64,3584]{2,1,0:T(8,128)(2,1)}, bf16[1,64,3584]{2,1,0:T(8,128)(2,1)S(1)}, u32[]{:S(2)}, u32[]{:S(2)}) %collective-permute-start.1) | collective-permute-done | bytes 458784 | tf_op jit(solution)/shard_map/ppermute | solution.py:9
  15.5 1.2 broadcast_in_dim.26
  16.8 22.9 %all-to-all-start.2 = ((bf16[48,2,3584]{2,1,0:T(2,128)(2,1)}), bf16[48,2,3584]{2,1,0:T(2,128)(2,1)S(1)}, u32[]{:S(2)}, u32[]{:S(2)}) async-start(bf16[48,2,3584]{2,1,0:T(2,128)(2,1)} %bitcast.8), calls=%async_computation.2 | async-start | bytes 1376256 | tf_op jit(solution)/shard_map/all_to_all | solution.py:78
  39.7 2.4 %collective-permute-start = (bf16[1,64,3584]{2,1,0:T(8,128)(2,1)S(1)}, bf16[1,64,3584]{2,1,0:T(8,128)(2,1)S(1)}, u32[]{:S(2)}, u32[]{:S(2)}) collective-permute-start(bf16[1,64,3584]{2,1,0:T(8,128)(2,1)S(1)} %copy-done.8), channel_id=1, source_target_pairs={{0,48},{48,96},{96,144},{144,192},{192,240},{240,288},{288,336},{3... | collective-permute-start | bytes 1376264 | tf_op jit(solution)/shard_map/ppermute | solution.py:9
  42.2 28.9 %collective-permute-done = bf16[1,64,3584]{2,1,0:T(8,128)(2,1)S(1)} collective-permute-done((bf16[1,64,3584]{2,1,0:T(8,128)(2,1)S(1)}, bf16[1,64,3584]{2,1,0:T(8,128)(2,1)S(1)}, u32[]{:S(2)}, u32[]{:S(2)}) %collective-permute-start) | collective-permute-done | bytes 458784 | tf_op jit(solution)/shard_map/ppermute | solution.py:9
  71.4 2.4 %all-to-all-done.2 = bf16[48,2,3584]{2,1,0:T(2,128)(2,1)S(1)} async-done(((bf16[48,2,3584]{2,1,0:T(2,128)(2,1)}), bf16[48,2,3584]{2,1,0:T(2,128)(2,1)S(1)}, u32[]{:S(2)}, u32[]{:S(2)}) %all-to-all-start.2) | async-done | bytes 688160 | tf_op jit(solution)/shard_map/all_to_all | solution.py:78
  73.8 1.2 broadcast_in_dim.23
  75.0 13.5 %all-to-all-start = ((bf16[48,2,3584]{2,1,0:T(2,128)(2,1)}), bf16[48,2,3584]{2,1,0:T(2,128)(2,1)S(1)}, u32[]{:S(2)}, u32[]{:S(2)}) async-start(bf16[48,2,3584]{2,1,0:T(2,128)(2,1)} %bitcast.1), calls=%async_computation | async-start | bytes 1376256 | tf_op jit(solution)/shard_map/all_to_all | solution.py:64
  89.3 0.7 copy-done.3
  90.1 1.9 convolution_convert_fusion
  91.9 1.1 reshape.60
  93.0 29.6 %all-to-all-done = bf16[48,2,3584]{2,1,0:T(2,128)(2,1)S(1)} async-done(((bf16[48,2,3584]{2,1,0:T(2,128)(2,1)}), bf16[48,2,3584]{2,1,0:T(2,128)(2,1)S(1)}, u32[]{:S(2)}, u32[]{:S(2)}) %all-to-all-start) | async-done | bytes 688160 | tf_op jit(solution)/shard_map/all_to_all | solution.py:64
  122.7 4.7 %all-to-all-start.3 = ((bf16[48,2,3584]{2,1,0:T(2,128)(2,1)}), bf16[48,2,3584]{2,1,0:T(2,128)(2,1)S(1)}, u32[]{:S(2)}, u32[]{:S(2)}) async-start(bf16[48,2,3584]{2,1,0:T(2,128)(2,1)} %reshape.60), calls=%async_computation.3 | async-start | bytes 1376256 | tf_op jit(solution)/shard_map/all_to_all | solution.py:94
  127.6 1.5 fusion.39
  129.2 1.8 convolution_convert_fusion.1
  131.0 1.1 reshape.54
  132.1 29.4 %all-to-all-done.3 = bf16[48,2,3584]{2,1,0:T(2,128)(2,1)S(1)} async-done(((bf16[48,2,3584]{2,1,0:T(2,128)(2,1)}), bf16[48,2,3584]{2,1,0:T(2,128)(2,1)S(1)}, u32[]{:S(2)}, u32[]{:S(2)}) %all-to-all-start.3) | async-done | bytes 688160 | tf_op jit(solution)/shard_map/all_to_all | solution.py:94
  161.5 4.7 %all-to-all-start.1 = ((bf16[48,2,3584]{2,1,0:T(2,128)(2,1)}), bf16[48,2,3584]{2,1,0:T(2,128)(2,1)S(1)}, u32[]{:S(2)}, u32[]{:S(2)}) async-start(bf16[48,2,3584]{2,1,0:T(2,128)(2,1)} %reshape.54), calls=%async_computation.1 | async-start | bytes 1376256 | tf_op jit(solution)/shard_map/all_to_all | solution.py:72
  167.2 33.1 %all-to-all-done.1 = bf16[48,2,3584]{2,1,0:T(2,128)(2,1)S(1)} async-done(((bf16[48,2,3584]{2,1,0:T(2,128)(2,1)}), bf16[48,2,3584]{2,1,0:T(2,128)(2,1)S(1)}, u32[]{:S(2)}, u32[]{:S(2)}) %all-to-all-start.1) | async-done | bytes 688160 | tf_op jit(solution)/shard_map/all_to_all | solution.py:72
  200.3 0.6 convert_reduce_fusion.1
  201.0 1.8 fusion.8
  202.8 1.8 fusion.7
  (35 shorter events, 2.9 us)
Async XLA Ops:
  0.6 88.3 %copy-start = (bf16[1,128,3584]{2,1,0:T(8,128)(2,1)S(1)}, bf16[1,128,3584]{2,1,0:T(8,128)(2,1)}, u32[]{:S(2)}) copy-start(bf16[1,128,3584]{2,1,0:T(8,128)(2,1)} %param.15) | copy-start | bytes 2752516
  0.6 14.6 %collective-permute-start.1 = (bf16[1,64,3584]{2,1,0:T(8,128)(2,1)}, bf16[1,64,3584]{2,1,0:T(8,128)(2,1)S(1)}, u32[]{:S(2)}, u32[]{:S(2)}) collective-permute-start(bf16[1,64,3584]{2,1,0:T(8,128)(2,1)} %param.12), channel_id=1, source_target_pairs={{0,720},{48,0},{96,48},{144,96},{192,144},{240,192},{288,240},{336... | collective-permute-start | bytes 1376264 | tf_op jit(solution)/shard_map/ppermute | solution.py:9
  15.5 24.1 %copy-start.8 = (bf16[1,64,3584]{2,1,0:T(8,128)(2,1)S(1)}, bf16[1,64,3584]{2,1,0:T(8,128)(2,1)}, u32[]{:S(2)}) copy-start(bf16[1,64,3584]{2,1,0:T(8,128)(2,1)} %param.10) | copy-start | bytes 1376260
  15.5 26.5 %copy-start.5 = (s32[1,1,3,2]{2,3,1,0:T(2,128)S(1)}, s32[1,1,3,2]{2,3,1,0:T(2,128)}, u32[]{:S(2)}) copy-start(s32[1,1,3,2]{2,3,1,0:T(2,128)} %param.16) | copy-start | bytes 76
  16.8 57.0 %all-to-all-start.2 = ((bf16[48,2,3584]{2,1,0:T(2,128)(2,1)}), bf16[48,2,3584]{2,1,0:T(2,128)(2,1)S(1)}, u32[]{:S(2)}, u32[]{:S(2)}) async-start(bf16[48,2,3584]{2,1,0:T(2,128)(2,1)} %bitcast.8), calls=%async_computation.2 | async-start | bytes 1376256 | tf_op jit(solution)/shard_map/all_to_all | solution.py:78
  39.7 31.5 %collective-permute-start = (bf16[1,64,3584]{2,1,0:T(8,128)(2,1)S(1)}, bf16[1,64,3584]{2,1,0:T(8,128)(2,1)S(1)}, u32[]{:S(2)}, u32[]{:S(2)}) collective-permute-start(bf16[1,64,3584]{2,1,0:T(8,128)(2,1)S(1)} %copy-done.8), channel_id=1, source_target_pairs={{0,48},{48,96},{96,144},{144,192},{192,240},{240,288},{288,336},{3... | collective-permute-start | bytes 1376264 | tf_op jit(solution)/shard_map/ppermute | solution.py:9
  71.1 3.9 %copy-start.1 = (bf16[1,64,3584]{2,1,0:T(8,128)(2,1)}, bf16[1,64,3584]{2,1,0:T(8,128)(2,1)S(1)}, u32[]{:S(2)}) copy-start(bf16[1,64,3584]{2,1,0:T(8,128)(2,1)S(1)} %collective-permute-done) | copy-start | bytes 1376260
  71.4 17.1 %copy-start.4 = (bf16[1,48,2,2,128]{4,3,2,1,0:T(2,128)(2,1)S(1)}, bf16[1,48,2,2,128]{4,3,2,1,0:T(2,128)(2,1)}, u32[]{:S(2)}) copy-start(bf16[1,48,2,2,128]{4,3,2,1,0:T(2,128)(2,1)} %param.11) | copy-start | bytes 147460
  75.0 47.7 %all-to-all-start = ((bf16[48,2,3584]{2,1,0:T(2,128)(2,1)}), bf16[48,2,3584]{2,1,0:T(2,128)(2,1)S(1)}, u32[]{:S(2)}, u32[]{:S(2)}) async-start(bf16[48,2,3584]{2,1,0:T(2,128)(2,1)} %bitcast.1), calls=%async_computation | async-start | bytes 1376256 | tf_op jit(solution)/shard_map/all_to_all | solution.py:64
  88.9 1.2 copy-start.3
  122.7 38.8 %all-to-all-start.3 = ((bf16[48,2,3584]{2,1,0:T(2,128)(2,1)}), bf16[48,2,3584]{2,1,0:T(2,128)(2,1)S(1)}, u32[]{:S(2)}, u32[]{:S(2)}) async-start(bf16[48,2,3584]{2,1,0:T(2,128)(2,1)} %reshape.60), calls=%async_computation.3 | async-start | bytes 1376256 | tf_op jit(solution)/shard_map/all_to_all | solution.py:94
  132.1 34.1 %copy-start.6 = (f32[1,1,3,2]{2,3,1,0:T(2,128)S(1)}, f32[1,1,3,2]{2,3,1,0:T(2,128)}, u32[]{:S(2)}) copy-start(f32[1,1,3,2]{2,3,1,0:T(2,128)} %param.19) | copy-start | bytes 76
  132.1 34.3 %copy-start.7 = (f32[1,1,3,2]{2,3,1,0:T(2,128)S(1)}, f32[1,1,3,2]{2,3,1,0:T(2,128)}, u32[]{:S(2)}) copy-start(f32[1,1,3,2]{2,3,1,0:T(2,128)} %param.17) | copy-start | bytes 76
  161.5 38.8 %all-to-all-start.1 = ((bf16[48,2,3584]{2,1,0:T(2,128)(2,1)}), bf16[48,2,3584]{2,1,0:T(2,128)(2,1)S(1)}, u32[]{:S(2)}, u32[]{:S(2)}) async-start(bf16[48,2,3584]{2,1,0:T(2,128)(2,1)} %reshape.54), calls=%async_computation.1 | async-start | bytes 1376256 | tf_op jit(solution)/shard_map/all_to_all | solution.py:72
  200.3 2.4 %copy-start.2 = (bf16[1,64,3584]{2,1,0:T(8,128)(2,1)S(1)}, bf16[1,64,3584]{2,1,0:T(8,128)(2,1)}, u32[]{:S(2)}) copy-start(bf16[1,64,3584]{2,1,0:T(8,128)(2,1)} %copy-done.1) | copy-start | bytes 1376260
where the time goes:
time: 205 us
  waiting for transfers between devices  129 us (63%)
  starting transfers between devices  56.5 us (28%)
  matrix products  9.67 us (5%)
  local copies, waits for them, and re-layouts  7.57 us (4%)
    ppermute x2, waiting for transfers between devices, shifted(): lax.ppermute(shard, axis, [(i, (i + by) % length) for i in range(length)])  34.2 us
    all_to_all x1, waiting for transfers between devices, local(): lax.all_to_all(partial_value.reshape(lead, items, width), 'expert', split...  33.1 us
    all_to_all x1, waiting for transfers between devices, local(): lax.all_to_all(fwd_send, 'expert', split_axis=0, concat_axis=0, tiled=True)  29.6 us
    all_to_all x1, waiting for transfers between devices, local(): lax.all_to_all(partial_value, 'expert', split_axis=0, concat_axis=0, tile...  29.4 us
    all_to_all x1, starting transfers between devices, local(): lax.all_to_all(grad_send, 'expert', split_axis=0, concat_axis=0, tiled=True)  22.9 us
    all_to_all x1, starting transfers between devices, local(): lax.all_to_all(fwd_send, 'expert', split_axis=0, concat_axis=0, tiled=True)  13.5 us
    ppermute x2, starting transfers between devices, shifted(): lax.ppermute(shard, axis, [(i, (i + by) % length) for i in range(length)])  10.8 us
    all_to_all x1, starting transfers between devices, local(): lax.all_to_all(partial_value.reshape(lead, items, width), 'expert', split...  4.67 us
  transfers between devices with their start and end apart: 6, of which 6 were waited for; matrix products, arithmetic and copies ran while one was open for 5% of the time, Pallas kernels for 0%

commit v1 on v0

v1 whole, which is shorter than its diff:
```python
import jax
import jax.numpy as jnp
from jax import lax
from jax.sharding import PartitionSpec as P

CORES = 2
HALVES = 2
GROUPS = 3


def shifted(shard, axis, by):
    length = lax.axis_size(axis)
    return lax.ppermute(shard, axis, [(i, (i + by) % length) for i in range(length)])


def layout(length):
    depth = length // (GROUPS * HALVES * CORES)

    def at(group, z, half, core):
        return ((group * depth + z) * HALVES + half) * CORES + core

    zs, halves, cores, groups = range(depth), range(HALVES), range(CORES), range(GROUPS)
    far = [[at(g, z, h, c) for g in groups for h in halves] for z in zs for c in cores]
    line = [[at(g, z, h, c) for z in zs] for g in groups for h in halves for c in cores]
    pair = [[at(g, z, h, c) for c in cores] for g in groups for z in zs for h in halves]
    return depth, far, line, pair


def pick_rows(slots, block):
    count = block.shape[0]
    flat = slots.reshape(-1)
    onehot = flat[:, None] == jnp.arange(count, dtype=jnp.int32)[None, :]
    rows = jnp.dot(onehot.astype(jnp.bfloat16), block, preferred_element_type=jnp.float32).astype(
        jnp.bfloat16
    )
    return (onehot.astype(jnp.float32), rows)


def settle(result, onehot, gates, block):
    weighted = onehot * gates.reshape(-1)[:, None]
    added = lax.dot_general(
        weighted, result, (((0,), (0,)), ((), ())), precision=lax.Precision.HIGHEST
    )
    return (block.astype(jnp.float32) + added).astype(jnp.bfloat16)


def local(
    fwd_held,
    saved_preact,
    grad_held,
    gate_weight,
    up_weight,
    down_weight,
    fwd_slots,
    fwd_gates,
    bwd_slots,
    bwd_gates,
):
    width = fwd_held.shape[2]
    cap = fwd_slots.shape[3]
    both = 2 * cap
    length = lax.axis_size("expert")
    depth, far, line, pair = layout(length)
    spokes = GROUPS * HALVES
    w_gate = gate_weight[0]
    w_up = up_weight[0]
    w_down = down_weight[0]
    hidden_width = w_down.shape[0]

    inputs = shifted(fwd_held, "section", 1)[0]
    incoming = shifted(grad_held, "section", -1)[0]

    saved = saved_preact[0].reshape(GROUPS, depth, HALVES, CORES, cap, 2, hidden_width)
    saved = saved.transpose(5, 3, 1, 0, 2, 4, 6)
    saved = jnp.concatenate([jnp.zeros_like(saved), saved], axis=5)
    saved = saved.reshape(2, -1, hidden_width).astype(jnp.float32)
    pre_a, pre_v = saved[0], saved[1]

    fwd_hot, fwd_rows = pick_rows(fwd_slots[0, 0], inputs)
    bwd_hot, bwd_rows = pick_rows(bwd_slots[0, 0], incoming)
    rows = jnp.concatenate(
        [fwd_rows.reshape(GROUPS, cap, width), bwd_rows.reshape(GROUPS, cap, width)], axis=1
    )
    rows = jnp.broadcast_to(rows[:, None], (GROUPS, HALVES, both, width)).reshape(spokes, both, width)
    rows = lax.all_to_all(rows, "expert", 0, 0, axis_index_groups=far, tiled=True)
    rows = rows.reshape(spokes * both, width)
    rows = lax.all_gather(rows, "expert", axis_index_groups=line, tiled=True)
    rows = lax.all_gather(rows, "expert", axis_index_groups=pair, tiled=True)

    pre_gate = jnp.dot(rows, w_gate, preferred_element_type=jnp.float32)
    pre_up = jnp.dot(rows, w_up, preferred_element_type=jnp.float32)
    dh = lax.dot_general(rows, w_down, (((1,), (1,)), ((), ())), preferred_element_type=jnp.float32)
    is_fwd = (lax.broadcasted_iota(jnp.int32, pre_gate.shape, 0) % both) < cap
    hidden = jnp.where(is_fwd, jax.nn.silu(pre_gate) * pre_up, 0.0)
    sig = jax.nn.sigmoid(pre_a)
    act = pre_a * sig
    slope = sig * (1.0 + pre_a * (1.0 - sig))
    acts = jnp.concatenate([hidden, dh * pre_v * slope, dh * act], axis=1).astype(jnp.bfloat16)
    w_out = jnp.concatenate([w_down, w_gate.T, w_up.T], axis=0)
    part = jnp.dot(acts, w_out, preferred_element_type=jnp.float32).astype(jnp.bfloat16)

    def summed(parts, members, groups):
        parts = parts.reshape(members, -1, width)
        parts = lax.all_to_all(parts, "expert", 0, 0, axis_index_groups=groups, tiled=True)
        return parts.astype(jnp.float32).sum(axis=0).astype(jnp.bfloat16)

    part = summed(part, CORES, pair)
    part = summed(part, depth, line)
    part = part.reshape(spokes, both, width)
    part = lax.all_to_all(part, "expert", 0, 0, axis_index_groups=far, tiled=True)
    part = part.astype(jnp.float32).reshape(GROUPS, HALVES, both, width).sum(axis=1)
    fwd_out = settle(part[:, :cap].reshape(-1, width), fwd_hot, fwd_gates[0, 0], inputs)
    grad_out = settle(part[:, cap:].reshape(-1, width), bwd_hot, bwd_gates[0, 0], incoming)
    return (fwd_out[None], grad_out[None])


def solution(mesh):
    in_specs = (
        P("section", "expert", None),
        P("section", None, None, None, "expert"),
        P("section", "expert", None),
        P("section", None, "expert"),
        P("section", None, "expert"),
        P("section", "expert", None),
        P("section", "expert", None, None),
        P("section", "expert", None, None),
        P("section", "expert", None, None),
        P("section", "expert", None, None),
    )
    out_specs = (P("section", "expert", None), P("section", "expert", None))
    return jax.shard_map(local, mesh=mesh, in_specs=in_specs, out_specs=out_specs, check_vma=False)
```

time: 205 us -> 166 us (0.81)
  the two profiles are of different devices: /device:TPU:1 before, /device:TPU:2 now
where the time goes in v1:
time: 166 us; the launch traced here: 165 us
  blocking collectives  76 us (46%)
  waiting for transfers between devices  34.2 us (21%)
  starting transfers between devices  25.4 us (15%)
  between operations  14.2 us (9%)
  matrix products  7.89 us (5%)
  local copies, waits for them, and re-layouts  6.74 us (4%)
    all_to_all x1, blocking collectives, local(): lax.all_to_all(rows, 'expert', 0, 0, axis_index_groups=far, tiled=True)  30.3 us
    all_to_all x2, blocking collectives, summed(): lax.all_to_all(parts, 'expert', 0, 0, axis_index_groups=groups, tiled=True)  28 us
    all_gather x1, blocking collectives, local(): rows = lax.all_gather(rows, 'expert', axis_index_groups=line, tiled=True)  17.7 us
    all_gather x1, waiting for transfers between devices, local(): rows = lax.all_gather(rows, 'expert', axis_index_groups=pair, tiled=True)  16 us
    all_to_all x1, waiting for transfers between devices, local(): lax.all_to_all(part, 'expert', 0, 0, axis_index_groups=far, tiled=True)  13.9 us
    ppermute x2, starting transfers between devices, shifted(): lax.ppermute(shard, axis, [(i, (i + by) % length) for i in range(length)])  13.4 us
    all_to_all x1, starting transfers between devices, local(): lax.all_to_all(part, 'expert', 0, 0, axis_index_groups=far, tiled=True)  12 us
    unnamed x24, local copies, waits for them, and re-layouts  5.24 us
  transfers between devices with their start and end apart: 4, of which 4 were waited for; matrix products, arithmetic and copies ran while one was open for 3% of the time, Pallas kernels for 0%

profile of v1, /device:TPU:2, one launch (start us, length us, event | category | flops | bytes accessed | tf_op | source)
XLA Modules:
  0.0 165.3 jit_solution(11493438575046093881)
XLA Ops:
  7.2 3.4 %collective-permute-start = (bf16[1,64,3584]{2,1,0:T(8,128)(2,1)}, bf16[1,64,3584]{2,1,0:T(8,128)(2,1)S(1)}, u32[]{:S(2)}, u32[]{:S(2)}) collective-permute-start(bf16[1,64,3584]{2,1,0:T(8,128)(2,1)} %param.10), channel_id=1, source_target_pairs={{0,48},{48,96},{96,144},{144,192},{192,240},{240,288},{288,336},{3... | collective-permute-start | bytes 1376264 | tf_op jit(solution)/shard_map/ppermute | solution.py:13
  10.6 10.0 %collective-permute-start.1 = (bf16[1,64,3584]{2,1,0:T(8,128)(2,1)}, bf16[1,64,3584]{2,1,0:T(8,128)(2,1)S(1)}, u32[]{:S(2)}, u32[]{:S(2)}) collective-permute-start(bf16[1,64,3584]{2,1,0:T(8,128)(2,1)} %param.12), channel_id=1, source_target_pairs={{0,720},{48,0},{96,48},{144,96},{192,144},{240,192},{288,240},{336... | collective-permute-start | bytes 1376264 | tf_op jit(solution)/shard_map/ppermute | solution.py:13
  20.6 0.8 copy.26
  21.4 0.8 copy.28
  22.3 3.0 %collective-permute-done = bf16[1,64,3584]{2,1,0:T(8,128)(2,1)S(1)} collective-permute-done((bf16[1,64,3584]{2,1,0:T(8,128)(2,1)}, bf16[1,64,3584]{2,1,0:T(8,128)(2,1)S(1)}, u32[]{:S(2)}, u32[]{:S(2)}) %collective-permute-start) | collective-permute-done | bytes 458784 | tf_op jit(solution)/shard_map/ppermute | solution.py:13
  25.6 1.3 collective-permute-done.1
  27.3 30.3 %all_to_all.20 = bf16[6,4,3584]{2,1,0:T(4,128)(2,1)S(1)} all-to-all(bf16[6,4,3584]{2,1,0:T(4,128)(2,1)S(1)} %bitcast.50), channel_id=1, replica_groups={{0,2,16,18,32,34},{1,3,17,19,33,35},{4,6,20,22,36,38},{5,7,21,23,37,39}..., dimensions={0} | all-to-all | bytes 344064 | tf_op jit(solution)/shard_map/all_to_all | solution.py:85
  57.7 17.7 %all_gather.6 = bf16[96,3584]{1,0:T(8,128)(2,1)} all-gather(bf16[24,3584]{1,0:T(8,128)(2,1)S(1)} %reshape.51), channel_id=1, replica_groups={{0,4,8,12},{1,5,9,13},{2,6,10,14},{3,7,11,15},{16,20,24,28},{17,21,25,2..., dimensions={0}, use_global_device_ids=true | all-gather | bytes 860160 | tf_op jit(solution)/shard_map/all_gather | solution.py:87
  75.5 1.3 copy.29
  76.8 1.3 copy.30
  78.1 16.0 %all-gather.2.cloned.1.call-done = bf16[192,3584]{1,0:T(8,128)(2,1)} async-done(((bf16[96,3584]{1,0:T(8,128)(2,1)}), bf16[192,3584]{1,0:T(8,128)(2,1)}) %all-gather.2.cloned.1.call-update) | async-done | bytes 1376272 | tf_op jit(solution)/shard_map/all_gather | solution.py:88
  94.1 2.0 %fusion.8 = f32[192,128]{1,0:T(8,128)S(1)} fusion(bf16[192,3584]{1,0:T(8,128)(2,1)} %all-gather.2.cloned.1.call-done, bf16[1,3584,128]{2,1,0:T(8,128)(2,1)S(1)} %copy-done), kind=kOutput, calls=%fused_computation.12 | convolution fusion | flops 176160768 | bytes 2392064 | tf_op jit(solution)/shard_map/dot_general | solution.py:90
  96.2 0.5 multiply_convert_fusion.1
  96.7 0.5 fusion.6
  97.2 0.6 copy-done.3
  98.1 0.9 convolution_convert_fusion
  99.0 4.8 %all_to_all.21 = bf16[2,96,3584]{2,1,0:T(8,128)(2,1)S(1)} all-to-all(bf16[2,96,3584]{2,1,0:T(8,128)(2,1)S(1)} %bitcast.46), channel_id=1, replica_groups={{0,1},{2,3},{4,5},{6,7},{8,9},{10,11},{12,13},{14,15},{16,17},{18,19},{..., dimensions={0} | all-to-all | bytes 2752512 | tf_op jit(solution)/shard_map/all_to_all | solution.py:104
  103.8 0.4 reduce_sum.33
  104.3 23.2 %all_to_all.22 = bf16[4,24,3584]{2,1,0:T(8,128)(2,1)S(1)} all-to-all(bf16[4,24,3584]{2,1,0:T(8,128)(2,1)S(1)} %bitcast.45), channel_id=1, replica_groups={{0,4,8,12},{1,5,9,13},{2,6,10,14},{3,7,11,15},{16,20,24,28},{17,21,25,2..., dimensions={0} | all-to-all | bytes 1376256 | tf_op jit(solution)/shard_map/all_to_all | solution.py:104
  127.6 0.7 reshape.54
  128.4 12.0 %all-to-all-start.3 = ((bf16[6,4,3584]{2,1,0:T(4,128)(2,1)}), bf16[6,4,3584]{2,1,0:T(4,128)(2,1)S(1)}, u32[]{:S(2)}, u32[]{:S(2)}) async-start(bf16[6,4,3584]{2,1,0:T(4,128)(2,1)} %reshape.54), calls=%async_computation.3 | async-start | bytes 344064 | tf_op jit(solution)/shard_map/all_to_all | solution.py:110
  140.7 13.9 %all-to-all-done.3 = bf16[6,4,3584]{2,1,0:T(4,128)(2,1)S(1)} async-done(((bf16[6,4,3584]{2,1,0:T(4,128)(2,1)}), bf16[6,4,3584]{2,1,0:T(4,128)(2,1)S(1)}, u32[]{:S(2)}, u32[]{:S(2)}) %all-to-all-start.3) | async-done | bytes 172064 | tf_op jit(solution)/shard_map/all_to_all | solution.py:110
  154.9 1.8 %fusion.11 = bf16[1,64,3584]{2,1,0:T(8,128)(2,1)} fusion(bf16[1,64,3584]{2,1,0:T(8,128)(2,1)S(1)} %collective-permute-done.1, f32[6,3584]{1,0:T(8,128)S(1)} %reshape.58, f32[6]{0:T(128)S(1)} %mul.56, s32[6]{0:T(128)S(1)} %eq.36), kind=kOutput, calls=%fused_computation.17 | convolution fusion | flops 17203968 | bytes 1003568 | tf_op jit(solution)/shard_map/dot_general | solution.py:41
  156.7 1.8 %fusion.10 = bf16[1,64,3584]{2,1,0:T(8,128)(2,1)} fusion(bf16[1,64,3584]{2,1,0:T(8,128)(2,1)S(1)} %collective-permute-done, f32[6,3584]{1,0:T(8,128)S(1)} %reshape.57, f32[6]{0:T(128)S(1)} %mul.45, s32[6]{0:T(128)S(1)} %eq.32), kind=kOutput, calls=%fused_computation.16 | convolution fusion | flops 17203968 | bytes 1003568 | tf_op jit(solution)/shard_map/dot_general | solution.py:41
  (42 shorter events, 2.2 us)
Async XLA Ops:
  7.2 87.0 %all-gather.2.cloned.1.call-start = ((), (), s32[]{:S(2)}) async-start(), calls=%async_computation.4 | async-start | bytes 2064384 | tf_op jit(solution)/shard_map/all_gather | solution.py:88
  7.2 18.1 %collective-permute-start = (bf16[1,64,3584]{2,1,0:T(8,128)(2,1)}, bf16[1,64,3584]{2,1,0:T(8,128)(2,1)S(1)}, u32[]{:S(2)}, u32[]{:S(2)}) collective-permute-start(bf16[1,64,3584]{2,1,0:T(8,128)(2,1)} %param.10), channel_id=1, source_target_pairs={{0,48},{48,96},{96,144},{144,192},{192,240},{240,288},{288,336},{3... | collective-permute-start | bytes 1376264 | tf_op jit(solution)/shard_map/ppermute | solution.py:13
  10.6 16.3 %collective-permute-start.1 = (bf16[1,64,3584]{2,1,0:T(8,128)(2,1)}, bf16[1,64,3584]{2,1,0:T(8,128)(2,1)S(1)}, u32[]{:S(2)}, u32[]{:S(2)}) collective-permute-start(bf16[1,64,3584]{2,1,0:T(8,128)(2,1)} %param.12), channel_id=1, source_target_pairs={{0,720},{48,0},{96,48},{144,96},{192,144},{240,192},{288,240},{336... | collective-permute-start | bytes 1376264 | tf_op jit(solution)/shard_map/ppermute | solution.py:13
  27.1 48.3 %copy-start.5 = (bf16[1,48,2,2,128]{4,3,2,1,0:T(2,128)(2,1)S(1)}, bf16[1,48,2,2,128]{4,3,2,1,0:T(2,128)(2,1)}, u32[]{:S(2)}) copy-start(bf16[1,48,2,2,128]{4,3,2,1,0:T(2,128)(2,1)} %param.11) | copy-start | bytes 147460
  27.2 48.3 %copy-start = (bf16[1,3584,128]{2,1,0:T(8,128)(2,1)S(1)}, bf16[1,3584,128]{2,1,0:T(8,128)(2,1)}, u32[]{:S(2)}) copy-start(bf16[1,3584,128]{2,1,0:T(8,128)(2,1)} %param.13) | copy-start | bytes 2752516
  75.4 1.4 copy-start.2
  94.1 2.0 %copy-start.1 = (bf16[192,3584]{1,0:T(8,128)(2,1)S(1)}, bf16[192,3584]{1,0:T(8,128)(2,1)}, u32[]{:S(2)}) copy-start(bf16[192,3584]{1,0:T(8,128)(2,1)} %all-gather.2.cloned.1.call-done) | copy-start | bytes 4128772
  94.1 2.0 %copy-start.8 = (bf16[1,128,3584]{2,1,0:T(8,128)(2,1)S(1)}, bf16[1,128,3584]{2,1,0:T(8,128)(2,1)}, u32[]{:S(2)}) copy-start(bf16[1,128,3584]{2,1,0:T(8,128)(2,1)} %param.15) | copy-start | bytes 2752516
  96.7 1.2 copy-start.3
  96.7 1.4 copy-start.4
  104.3 36.0 %copy-start.6 = (f32[1,1,3,2]{2,3,1,0:T(2,128)S(1)}, f32[1,1,3,2]{2,3,1,0:T(2,128)}, u32[]{:S(2)}) copy-start(f32[1,1,3,2]{2,3,1,0:T(2,128)} %param.19) | copy-start | bytes 76
  104.3 36.2 %copy-start.7 = (f32[1,1,3,2]{2,3,1,0:T(2,128)S(1)}, f32[1,1,3,2]{2,3,1,0:T(2,128)}, u32[]{:S(2)}) copy-start(f32[1,1,3,2]{2,3,1,0:T(2,128)} %param.17) | copy-start | bytes 76
  128.4 26.2 %all-to-all-start.3 = ((bf16[6,4,3584]{2,1,0:T(4,128)(2,1)}), bf16[6,4,3584]{2,1,0:T(4,128)(2,1)S(1)}, u32[]{:S(2)}, u32[]{:S(2)}) async-start(bf16[6,4,3584]{2,1,0:T(4,128)(2,1)} %reshape.54), calls=%async_computation.3 | async-start | bytes 344064 | tf_op jit(solution)/shard_map/all_to_all | solution.py:110
Sparse Core Ops, SparseCore 0:
  75.5 18.5 all-gather.1

commit v2 on v1

v2 whole, which is shorter than its diff:
```python
import jax
import jax.numpy as jnp
from jax import lax
from jax.sharding import PartitionSpec as P

CORES = 2
GROUPS = 3


def shifted(shard, axis, by):
    length = lax.axis_size(axis)
    return lax.ppermute(shard, axis, [(i, (i + by) % length) for i in range(length)])


def swapped(shard, axis):
    length = lax.axis_size(axis)
    return lax.ppermute(shard, axis, [(i, i ^ 1) for i in range(length)])


def pick_rows(slots, block):
    count = block.shape[0]
    flat = slots.reshape(-1)
    onehot = flat[:, None] == jnp.arange(count, dtype=jnp.int32)[None, :]
    rows = jnp.dot(onehot.astype(jnp.bfloat16), block, preferred_element_type=jnp.float32).astype(
        jnp.bfloat16
    )
    return (onehot.astype(jnp.float32), rows)


def settle(result, onehot, gates, block):
    weighted = onehot * gates.reshape(-1)[:, None]
    added = lax.dot_general(
        weighted, result, (((0,), (0,)), ((), ())), precision=lax.Precision.HIGHEST
    )
    return (block.astype(jnp.float32) + added).astype(jnp.bfloat16)


def local(
    fwd_held,
    saved_preact,
    grad_held,
    gate_weight,
    up_weight,
    down_weight,
    fwd_slots,
    fwd_gates,
    bwd_slots,
    bwd_gates,
):
    width = fwd_held.shape[2]
    cap = fwd_slots.shape[3]
    both = 2 * cap
    length = lax.axis_size("expert")
    chips = length // CORES
    same_core = [[chip * CORES + core for chip in range(chips)] for core in range(CORES)]
    core = lax.axis_index("expert") % CORES
    w_gate = gate_weight[0]
    w_up = up_weight[0]
    w_down = down_weight[0]
    hidden_width = w_down.shape[0]

    inputs = shifted(fwd_held, "section", 1)[0]
    incoming = shifted(grad_held, "section", -1)[0]

    saved = saved_preact[0].reshape(chips, CORES, cap, 2, hidden_width)

    def saved_of(which):
        part = lax.dynamic_index_in_dim(saved, which, 1, keepdims=False)
        part = jnp.concatenate([jnp.zeros_like(part), part], axis=1)
        part = part.transpose(2, 0, 1, 3).reshape(2, -1, hidden_width).astype(jnp.float32)
        return part[0], part[1]

    fwd_hot, fwd_rows = pick_rows(fwd_slots[0, 0], inputs)
    bwd_hot, bwd_rows = pick_rows(bwd_slots[0, 0], incoming)
    rows = jnp.concatenate(
        [fwd_rows.reshape(GROUPS, cap, width), bwd_rows.reshape(GROUPS, cap, width)], axis=1
    )
    rows = jnp.broadcast_to(rows[:, None], (GROUPS, chips // GROUPS, both, width))
    rows = rows.reshape(chips, both, width)
    rows = lax.all_to_all(rows, "expert", 0, 0, axis_index_groups=same_core, tiled=True)
    mine = rows.reshape(chips * both, width)
    other = swapped(mine, "expert")

    def expert(rows, pre_a, pre_v):
        pre_gate = jnp.dot(rows, w_gate, preferred_element_type=jnp.float32)
        pre_up = jnp.dot(rows, w_up, preferred_element_type=jnp.float32)
        dh = lax.dot_general(rows, w_down, (((1,), (1,)), ((), ())), preferred_element_type=jnp.float32)
        is_fwd = (lax.broadcasted_iota(jnp.int32, pre_gate.shape, 0) % both) < cap
        hidden = jnp.where(is_fwd, jax.nn.silu(pre_gate) * pre_up, 0.0)
        sig = jax.nn.sigmoid(pre_a)
        act = pre_a * sig
        slope = sig * (1.0 + pre_a * (1.0 - sig))
        acts = jnp.concatenate([hidden, dh * pre_v * slope, dh * act], axis=1).astype(jnp.bfloat16)
        w_out = jnp.concatenate([w_down, w_gate.T, w_up.T], axis=0)
        return jnp.dot(acts, w_out, preferred_element_type=jnp.float32).astype(jnp.bfloat16)

    away = swapped(expert(other, *saved_of(1 - core)), "expert")
    home = expert(mine, *saved_of(core))
    part = (home.astype(jnp.float32) + away.astype(jnp.float32)).astype(jnp.bfloat16)
    part = part.reshape(chips, both, width)
    part = lax.all_to_all(part, "expert", 0, 0, axis_index_groups=same_core, tiled=True)
    part = part.astype(jnp.float32).reshape(GROUPS, chips // GROUPS, both, width).sum(axis=1)
    fwd_out = settle(part[:, :cap].reshape(-1, width), fwd_hot, fwd_gates[0, 0], inputs)
    grad_out = settle(part[:, cap:].reshape(-1, width), bwd_hot, bwd_gates[0, 0], incoming)
    return (fwd_out[None], grad_out[None])


def solution(mesh):
    in_specs = (
        P("section", "expert", None),
        P("section", None, None, None, "expert"),
        P("section", "expert", None),
        P("section", None, "expert"),
        P("section", None, "expert"),
        P("section", "expert", None),
        P("section", "expert", None, None),
        P("section", "expert", None, None),
        P("section", "expert", None, None),
        P("section", "expert", None, None),
    )
    out_specs = (P("section", "expert", None), P("section", "expert", None))
    return jax.shard_map(local, mesh=mesh, in_specs=in_specs, out_specs=out_specs, check_vma=False)
```

time: 166 us -> 130 us (0.78)
  the two profiles are of different devices: /device:TPU:2 before, /device:TPU:30 now
where the time goes in v2:
time: 130 us
  waiting for transfers between devices  73.4 us (56%)
  starting transfers between devices  38.5 us (30%)
  local copies, waits for them, and re-layouts  9.01 us (7%)
  matrix products  7.56 us (6%)
    all_to_all x1, waiting for transfers between devices, local(): lax.all_to_all(part, 'expert', 0, 0, axis_index_groups=same_core, tiled=T...  31.4 us
    all_to_all x1, waiting for transfers between devices, local(): lax.all_to_all(rows, 'expert', 0, 0, axis_index_groups=same_core, tiled=T...  30.9 us
    all_to_all x1, starting transfers between devices, local(): lax.all_to_all(rows, 'expert', 0, 0, axis_index_groups=same_core, tiled=T...  15.1 us
    ppermute x2, starting transfers between devices, shifted(): lax.ppermute(shard, axis, [(i, (i + by) % length) for i in range(length)])  13 us
    ppermute x2, waiting for transfers between devices, shifted(): lax.ppermute(shard, axis, [(i, (i + by) % length) for i in range(length)])  10.6 us
    unnamed x30, local copies, waits for them, and re-layouts  6.05 us
    all_to_all x1, starting transfers between devices, local(): lax.all_to_all(part, 'expert', 0, 0, axis_index_groups=same_core, tiled=T...  6.04 us
    ppermute x2, starting transfers between devices, swapped(): return lax.ppermute(shard, axis, [(i, i ^ 1) for i in range(length)])  4.33 us
  transfers between devices with their start and end apart: 6, of which 5 were waited for; matrix products, arithmetic and copies ran while one was open for 5% of the time, Pallas kernels for 0%

profile of v2, /device:TPU:30, one launch (start us, length us, event | category | flops | bytes accessed | tf_op | source)
XLA Modules:
  0.0 129.9 jit_solution(14928462801958695311)
XLA Ops:
  0.6 11.1 %collective-permute-start = (bf16[1,64,3584]{2,1,0:T(8,128)(2,1)}, bf16[1,64,3584]{2,1,0:T(8,128)(2,1)S(1)}, u32[]{:S(2)}, u32[]{:S(2)}) collective-permute-start(bf16[1,64,3584]{2,1,0:T(8,128)(2,1)} %param.10), channel_id=1, source_target_pairs={{0,48},{48,96},{96,144},{144,192},{192,240},{240,288},{288,336},{3... | collective-permute-start | bytes 1376264 | tf_op jit(solution)/shard_map/ppermute | solution.py:12
  11.7 1.9 %collective-permute-start.1 = (bf16[1,64,3584]{2,1,0:T(8,128)(2,1)}, bf16[1,64,3584]{2,1,0:T(8,128)(2,1)S(1)}, u32[]{:S(2)}, u32[]{:S(2)}) collective-permute-start(bf16[1,64,3584]{2,1,0:T(8,128)(2,1)} %param.12), channel_id=1, source_target_pairs={{0,720},{48,0},{96,48},{144,96},{192,144},{240,192},{288,240},{336... | collective-permute-start | bytes 1376264 | tf_op jit(solution)/shard_map/ppermute | solution.py:12
  13.6 0.8 copy.20
  14.5 0.8 copy.22
  15.3 2.7 %collective-permute-done = bf16[1,64,3584]{2,1,0:T(8,128)(2,1)S(1)} collective-permute-done((bf16[1,64,3584]{2,1,0:T(8,128)(2,1)}, bf16[1,64,3584]{2,1,0:T(8,128)(2,1)S(1)}, u32[]{:S(2)}, u32[]{:S(2)}) %collective-permute-start) | collective-permute-done | bytes 458784 | tf_op jit(solution)/shard_map/ppermute | solution.py:12
  18.3 7.9 %collective-permute-done.1 = bf16[1,64,3584]{2,1,0:T(8,128)(2,1)S(1)} collective-permute-done((bf16[1,64,3584]{2,1,0:T(8,128)(2,1)}, bf16[1,64,3584]{2,1,0:T(8,128)(2,1)S(1)}, u32[]{:S(2)}, u32[]{:S(2)}) %collective-permute-start.1) | collective-permute-done | bytes 458784 | tf_op jit(solution)/shard_map/ppermute | solution.py:12
  26.6 1.0 broadcast_in_dim.19
  27.6 15.1 %all-to-all-start = ((bf16[24,4,3584]{2,1,0:T(4,128)(2,1)}), bf16[24,4,3584]{2,1,0:T(4,128)(2,1)S(1)}, u32[]{:S(2)}, u32[]{:S(2)}) async-start(bf16[24,4,3584]{2,1,0:T(4,128)(2,1)} %bitcast.2), calls=%async_computation | async-start | bytes 1376256 | tf_op jit(solution)/shard_map/all_to_all | solution.py:80
  42.9 30.9 %all-to-all-done = bf16[24,4,3584]{2,1,0:T(4,128)(2,1)S(1)} async-done(((bf16[24,4,3584]{2,1,0:T(4,128)(2,1)}), bf16[24,4,3584]{2,1,0:T(4,128)(2,1)S(1)}, u32[]{:S(2)}, u32[]{:S(2)}) %all-to-all-start) | async-done | bytes 688160 | tf_op jit(solution)/shard_map/all_to_all | solution.py:80
  73.9 1.9 %collective-permute-start.2 = (bf16[96,3584]{1,0:T(8,128)(2,1)S(1)}, bf16[96,3584]{1,0:T(8,128)(2,1)S(1)}, u32[]{:S(2)}, u32[]{:S(2)}) collective-permute-start(bf16[96,3584]{1,0:T(8,128)(2,1)S(1)} %reshape.51), channel_id=1, source_target_pairs={{0,1},{1,0},{2,3},{3,2},{4,5},{5,4},{6,7},{7,6},{8,9},{9,8},{10,11... | collective-permute-start | bytes 2064392 | tf_op jit(solution)/shard_map/ppermute | solution.py:17
  75.9 1.3 copy.23
  77.2 1.3 %copy.24 = bf16[1,3584,128]{1,2,0:T(8,128)(2,1)} copy(bf16[1,3584,128]{2,1,0:T(8,128)(2,1)S(1)} %copy-done.1) | data formatting | bytes 1835008 | tf_op args[4]
  79.0 0.8 copy-done.2
  81.0 0.5 copy-done.7
  81.5 0.6 convolution_convert_fusion
  82.1 2.4 %collective-permute-start.3 = (bf16[96,3584]{1,0:T(8,128)(2,1)S(1)}, bf16[96,3584]{1,0:T(8,128)(2,1)S(1)}, u32[]{:S(2)}, u32[]{:S(2)}) collective-permute-start(bf16[96,3584]{1,0:T(8,128)(2,1)S(1)} %convolution_convert_fusion), channel_id=1, source_target_pairs={{0,1},{1,0},{2,3},{3,2},{4,5},{5,4},{6,7},{7,6},{8,9},{9,8},{10,11... | collective-permute-start | bytes 2064392 | tf_op jit(solution)/shard_map/ppermute | solution.py:17
  85.2 0.4 multiply_convert_fusion.3
  85.7 0.6 collective-permute-done.3
  86.3 0.6 add_convert_fusion
  86.9 1.0 reshape.52
  88.0 6.0 %all-to-all-start.1 = ((bf16[24,4,3584]{2,1,0:T(4,128)(2,1)}), bf16[24,4,3584]{2,1,0:T(4,128)(2,1)S(1)}, u32[]{:S(2)}, u32[]{:S(2)}) async-start(bf16[24,4,3584]{2,1,0:T(4,128)(2,1)} %reshape.52), calls=%async_computation.1 | async-start | bytes 1376256 | tf_op jit(solution)/shard_map/all_to_all | solution.py:101
  94.4 31.4 %all-to-all-done.1 = bf16[24,4,3584]{2,1,0:T(4,128)(2,1)S(1)} async-done(((bf16[24,4,3584]{2,1,0:T(4,128)(2,1)}), bf16[24,4,3584]{2,1,0:T(4,128)(2,1)S(1)}, u32[]{:S(2)}, u32[]{:S(2)}) %all-to-all-start.1) | async-done | bytes 688160 | tf_op jit(solution)/shard_map/all_to_all | solution.py:101
  126.3 1.8 %fusion.11 = bf16[1,64,3584]{2,1,0:T(8,128)(2,1)} fusion(bf16[1,64,3584]{2,1,0:T(8,128)(2,1)S(1)} %copy-done.6, f32[6,3584]{1,0:T(8,128)S(1)} %reshape.56, f32[6]{0:T(128)S(1)} %mul.88, s32[6]{0:T(128)S(1)} %eq.39), kind=kOutput, calls=%fused_computation.21 | convolution fusion | flops 17203968 | bytes 1003568 | tf_op jit(solution)/shard_map/dot_general | solution.py:32
  128.1 1.8 %fusion.10 = bf16[1,64,3584]{2,1,0:T(8,128)(2,1)} fusion(bf16[1,64,3584]{2,1,0:T(8,128)(2,1)S(1)} %copy-done.4, f32[6,3584]{1,0:T(8,128)S(1)} %reshape.55, f32[6]{0:T(128)S(1)} %mul.69, s32[6]{0:T(128)S(1)} %eq.35), kind=kOutput, calls=%fused_computation.20 | convolution fusion | flops 17203968 | bytes 1003568 | tf_op jit(solution)/shard_map/dot_general | solution.py:32
  (52 shorter events, 4.3 us)
Async XLA Ops:
  0.6 17.4 %collective-permute-start = (bf16[1,64,3584]{2,1,0:T(8,128)(2,1)}, bf16[1,64,3584]{2,1,0:T(8,128)(2,1)S(1)}, u32[]{:S(2)}, u32[]{:S(2)}) collective-permute-start(bf16[1,64,3584]{2,1,0:T(8,128)(2,1)} %param.10), channel_id=1, source_target_pairs={{0,48},{48,96},{96,144},{144,192},{192,240},{240,288},{288,336},{3... | collective-permute-start | bytes 1376264 | tf_op jit(solution)/shard_map/ppermute | solution.py:12
  11.7 14.5 %collective-permute-start.1 = (bf16[1,64,3584]{2,1,0:T(8,128)(2,1)}, bf16[1,64,3584]{2,1,0:T(8,128)(2,1)S(1)}, u32[]{:S(2)}, u32[]{:S(2)}) collective-permute-start(bf16[1,64,3584]{2,1,0:T(8,128)(2,1)} %param.12), channel_id=1, source_target_pairs={{0,720},{48,0},{96,48},{144,96},{192,144},{240,192},{288,240},{336... | collective-permute-start | bytes 1376264 | tf_op jit(solution)/shard_map/ppermute | solution.py:12
  18.0 9.6 %copy-start.3 = (bf16[1,64,3584]{2,1,0:T(8,128)(2,1)}, bf16[1,64,3584]{2,1,0:T(8,128)(2,1)S(1)}, u32[]{:S(2)}) copy-start(bf16[1,64,3584]{2,1,0:T(8,128)(2,1)S(1)} %collective-permute-done) | copy-start | bytes 1376260
  26.2 1.4 %copy-start.5 = (bf16[1,64,3584]{2,1,0:T(8,128)(2,1)}, bf16[1,64,3584]{2,1,0:T(8,128)(2,1)S(1)}, u32[]{:S(2)}) copy-start(bf16[1,64,3584]{2,1,0:T(8,128)(2,1)S(1)} %collective-permute-done.1) | copy-start | bytes 1376260
  26.6 16.2 %copy-start.9 = (bf16[1,48,2,2,128]{4,3,2,1,0:T(2,128)(2,1)S(1)}, bf16[1,48,2,2,128]{4,3,2,1,0:T(2,128)(2,1)}, u32[]{:S(2)}) copy-start(bf16[1,48,2,2,128]{4,3,2,1,0:T(2,128)(2,1)} %param.11) | copy-start | bytes 147460
  27.6 46.1 %all-to-all-start = ((bf16[24,4,3584]{2,1,0:T(4,128)(2,1)}), bf16[24,4,3584]{2,1,0:T(4,128)(2,1)S(1)}, u32[]{:S(2)}, u32[]{:S(2)}) async-start(bf16[24,4,3584]{2,1,0:T(4,128)(2,1)} %bitcast.2), calls=%async_computation | async-start | bytes 1376256 | tf_op jit(solution)/shard_map/all_to_all | solution.py:80
  42.8 33.1 %copy-start = (bf16[1,3584,128]{2,1,0:T(8,128)(2,1)S(1)}, bf16[1,3584,128]{2,1,0:T(8,128)(2,1)}, u32[]{:S(2)}) copy-start(bf16[1,3584,128]{2,1,0:T(8,128)(2,1)} %param.13) | copy-start | bytes 2752516
  73.9 4.7 %collective-permute-start.2 = (bf16[96,3584]{1,0:T(8,128)(2,1)S(1)}, bf16[96,3584]{1,0:T(8,128)(2,1)S(1)}, u32[]{:S(2)}, u32[]{:S(2)}) collective-permute-start(bf16[96,3584]{1,0:T(8,128)(2,1)S(1)} %reshape.51), channel_id=1, source_target_pairs={{0,1},{1,0},{2,3},{3,2},{4,5},{5,4},{6,7},{7,6},{8,9},{9,8},{10,11... | collective-permute-start | bytes 2064392 | tf_op jit(solution)/shard_map/ppermute | solution.py:17
  75.9 1.3 %copy-start.1 = (bf16[1,3584,128]{2,1,0:T(8,128)(2,1)S(1)}, bf16[1,3584,128]{2,1,0:T(8,128)(2,1)}, u32[]{:S(2)}) copy-start(bf16[1,3584,128]{2,1,0:T(8,128)(2,1)} %param.14) | copy-start | bytes 2752516
  78.6 1.2 copy-start.2
  79.8 1.2 copy-start.8
  80.2 1.3 copy-start.7
  82.1 4.2 %collective-permute-start.3 = (bf16[96,3584]{1,0:T(8,128)(2,1)S(1)}, bf16[96,3584]{1,0:T(8,128)(2,1)S(1)}, u32[]{:S(2)}, u32[]{:S(2)}) collective-permute-start(bf16[96,3584]{1,0:T(8,128)(2,1)S(1)} %convolution_convert_fusion), channel_id=1, source_target_pairs={{0,1},{1,0},{2,3},{3,2},{4,5},{5,4},{6,7},{7,6},{8,9},{9,8},{10,11... | collective-permute-start | bytes 2064392 | tf_op jit(solution)/shard_map/ppermute | solution.py:17
  87.9 6.0 %copy-start.10 = (f32[1,1,3,2]{2,3,1,0:T(2,128)S(1)}, f32[1,1,3,2]{2,3,1,0:T(2,128)}, u32[]{:S(2)}) copy-start(f32[1,1,3,2]{2,3,1,0:T(2,128)} %param.17) | copy-start | bytes 76
  87.9 6.2 %copy-start.11 = (f32[1,1,3,2]{2,3,1,0:T(2,128)S(1)}, f32[1,1,3,2]{2,3,1,0:T(2,128)}, u32[]{:S(2)}) copy-start(f32[1,1,3,2]{2,3,1,0:T(2,128)} %param.19) | copy-start | bytes 76
  88.0 37.8 %all-to-all-start.1 = ((bf16[24,4,3584]{2,1,0:T(4,128)(2,1)}), bf16[24,4,3584]{2,1,0:T(4,128)(2,1)S(1)}, u32[]{:S(2)}, u32[]{:S(2)}) async-start(bf16[24,4,3584]{2,1,0:T(4,128)(2,1)} %reshape.52), calls=%async_computation.1 | async-start | bytes 1376256 | tf_op jit(solution)/shard_map/all_to_all | solution.py:101
  94.0 32.3 %copy-start.6 = (bf16[1,64,3584]{2,1,0:T(8,128)(2,1)S(1)}, bf16[1,64,3584]{2,1,0:T(8,128)(2,1)}, u32[]{:S(2)}) copy-start(bf16[1,64,3584]{2,1,0:T(8,128)(2,1)} %copy-done.5) | copy-start | bytes 1376260
  126.1 2.0 %copy-start.4 = (bf16[1,64,3584]{2,1,0:T(8,128)(2,1)S(1)}, bf16[1,64,3584]{2,1,0:T(8,128)(2,1)}, u32[]{:S(2)}) copy-start(bf16[1,64,3584]{2,1,0:T(8,128)(2,1)} %copy-done.3) | copy-start | bytes 1376260

commit v3 on v2

--- a/solution.py
+++ b/solution.py
@@ -1,6 +1,8 @@
 import jax
 import jax.numpy as jnp
 from jax import lax
+from jax.experimental import pallas as pl
+from jax.experimental.pallas import tpu as pltpu
 from jax.sharding import PartitionSpec as P
 
 CORES = 2
@@ -18,21 +20,53 @@
 
 
 def pick_rows(slots, block):
-    count = block.shape[0]
-    flat = slots.reshape(-1)
-    onehot = flat[:, None] == jnp.arange(count, dtype=jnp.int32)[None, :]
-    rows = jnp.dot(onehot.astype(jnp.bfloat16), block, preferred_element_type=jnp.float32).astype(
+    onehot = slots[:, None] == jnp.arange(block.shape[0], dtype=jnp.int32)[None, :]
+    return jnp.dot(onehot.astype(jnp.bfloat16), block, preferred_element_type=jnp.float32).astype(
         jnp.bfloat16
     )
-    return (onehot.astype(jnp.float32), rows)
 
 
-def settle(result, onehot, gates, block):
-    weighted = onehot * gates.reshape(-1)[:, None]
-    added = lax.dot_general(
-        weighted, result, (((0,), (0,)), ((), ())), precision=lax.Precision.HIGHEST
-    )
-    return (block.astype(jnp.float32) + added).astype(jnp.bfloat16)
+def settle_kernel(
+    fwd_slots, fwd_gates, bwd_slots, bwd_gates, back, inputs, incoming, fwd_out, grad_out, total
+):
+    chips, both, _ = back.shape
+    cap = both // 2
+    pieces = chips // GROUPS
+    tokens = inputs.shape[0]
+    sums = []
+    for group in range(GROUPS):
+        acc = back[group * pieces].astype(jnp.float32)
+        for piece in range(1, pieces):
+            acc = acc + back[group * pieces + piece].astype(jnp.float32)
+        sums.append(acc)
+    jobs = ((fwd_slots, fwd_gates, inputs, fwd_out, 0), (bwd_slots, bwd_gates, incoming, grad_out, cap))
+    for slots, gates, block, out, first in jobs:
+        total[:tokens] = block[...].astype(jnp.float32)
+        for group in range(GROUPS):
+            for slot in range(cap):
+                row = pl.ds(slots[group * cap + slot], 1)
+                piece = sums[group][first + slot : first + slot + 1]
+                total[row] = total[row] + gates[group * cap + slot] * piece
+        out[...] = total[:tokens].astype(out.dtype)
+
+
+def settle(back, fwd_slots, fwd_gates, inputs, bwd_slots, bwd_gates, incoming):
+    chips, both, width = back.shape
+    tokens = inputs.shape[0]
+    step = width // 4
+    smem = pl.BlockSpec(memory_space=pltpu.SMEM)
+    rows = pl.BlockSpec((tokens, step), lambda i: (0, i))
+    return pl.pallas_call(
+        settle_kernel,
+        grid=(width // step,),
+        out_shape=[jax.ShapeDtypeStruct((tokens, width), jnp.bfloat16)] * 2,
+        in_specs=[smem] * 4 + [pl.BlockSpec((chips, both, step), lambda i: (0, 0, i)), rows, rows],
+        out_specs=[rows, rows],
+        scratch_shapes=[pltpu.VMEM((tokens + 8, step), jnp.float32)],
+        compiler_params=pltpu.CompilerParams(vmem_limit_bytes=16 * 1024 * 1024),
+        cost_estimate=pl.CostEstimate(flops=2 * chips * both * width, bytes_accessed=2560 * width // 4, transcendentals=0),
+        name="settle",
+    )(fwd_slots, fwd_gates, bwd_slots, bwd_gates, back, inputs, incoming)
 
 
 def local(
@@ -61,6 +95,8 @@
 
     inputs = shifted(fwd_held, "section", 1)[0]
     incoming = shifted(grad_held, "section", -1)[0]
+    fwd_index = fwd_slots.reshape(-1)
+    bwd_index = bwd_slots.reshape(-1)
 
     saved = saved_preact[0].reshape(chips, CORES, cap, 2, hidden_width)
 
@@ -70,13 +106,17 @@
         part = part.transpose(2, 0, 1, 3).reshape(2, -1, hidden_width).astype(jnp.float32)
         return part[0], part[1]
 
-    fwd_hot, fwd_rows = pick_rows(fwd_slots[0, 0], inputs)
-    bwd_hot, bwd_rows = pick_rows(bwd_slots[0, 0], incoming)
+    saves = (*saved_of(core), *saved_of(1 - core))
+    w_out = jnp.concatenate([w_down, w_gate.T, w_up.T], axis=0)
+
+    fwd_rows = pick_rows(fwd_index, inputs)
+    bwd_rows = pick_rows(bwd_index, incoming)
     rows = jnp.concatenate(
         [fwd_rows.reshape(GROUPS, cap, width), bwd_rows.reshape(GROUPS, cap, width)], axis=1
     )
     rows = jnp.broadcast_to(rows[:, None], (GROUPS, chips // GROUPS, both, width))
     rows = rows.reshape(chips, both, width)
+    rows, w_out, saves = lax.optimization_barrier((rows, w_out, saves))
     rows = lax.all_to_all(rows, "expert", 0, 0, axis_index_groups=same_core, tiled=True)
     mine = rows.reshape(chips * both, width)
     other = swapped(mine, "expert")
@@ -91,17 +131,16 @@
         act = pre_a * sig
         slope = sig * (1.0 + pre_a * (1.0 - sig))
         acts = jnp.concatenate([hidden, dh * pre_v * slope, dh * act], axis=1).astype(jnp.bfloat16)
-        w_out = jnp.concatenate([w_down, w_gate.T, w_up.T], axis=0)
         return jnp.dot(acts, w_out, preferred_element_type=jnp.float32).astype(jnp.bfloat16)
 
-    away = swapped(expert(other, *saved_of(1 - core)), "expert")
-    home = expert(mine, *saved_of(core))
+    away = swapped(expert(other, *saves[2:]), "expert")
+    home = expert(mine, *saves[:2])
     part = (home.astype(jnp.float32) + away.astype(jnp.float32)).astype(jnp.bfloat16)
     part = part.reshape(chips, both, width)
     part = lax.all_to_all(part, "expert", 0, 0, axis_index_groups=same_core, tiled=True)
-    part = part.astype(jnp.float32).reshape(GROUPS, chips // GROUPS, both, width).sum(axis=1)
-    fwd_out = settle(part[:, :cap].reshape(-1, width), fwd_hot, fwd_gates[0, 0], inputs)
-    grad_out = settle(part[:, cap:].reshape(-1, width), bwd_hot, bwd_gates[0, 0], incoming)
+    fwd_out, grad_out = settle(
+        part, fwd_index, fwd_gates.reshape(-1), inputs, bwd_index, bwd_gates.reshape(-1), incoming
+    )
     return (fwd_out[None], grad_out[None])
 
 

time: 130 us -> 130 us (level)
  the two profiles are of different devices: /device:TPU:30 before, /device:TPU:64 now
where the time goes in v3:
time: 130 us
  blocking collectives  46.5 us (36%)
  waiting for transfers between devices  42 us (32%)
  starting transfers between devices  21.8 us (17%)
  local copies, waits for them, and re-layouts  8.04 us (6%)
  matrix products  5.21 us (4%)
  other arithmetic  3.08 us (2%)
  Pallas kernels  2.4 us (2%)
    all_to_all x1, blocking collectives, local(): lax.all_to_all(rows, 'expert', 0, 0, axis_index_groups=same_core, tiled=T...  46.5 us
    all_to_all x1, waiting for transfers between devices, local(): lax.all_to_all(part, 'expert', 0, 0, axis_index_groups=same_core, tiled=T...  31.1 us
    ppermute x2, starting transfers between devices, shifted(): lax.ppermute(shard, axis, [(i, (i + by) % length) for i in range(length)])  9.76 us
    ppermute x2, waiting for transfers between devices, shifted(): lax.ppermute(shard, axis, [(i, (i + by) % length) for i in range(length)])  7.91 us
    all_to_all x1, starting transfers between devices, local(): lax.all_to_all(part, 'expert', 0, 0, axis_index_groups=same_core, tiled=T...  7.86 us
    ppermute x2, starting transfers between devices, swapped(): return lax.ppermute(shard, axis, [(i, i ^ 1) for i in range(length)])  4.23 us
    unnamed x26, local copies, waits for them, and re-layouts  4.12 us
    ppermute x2, waiting for transfers between devices, swapped(): return lax.ppermute(shard, axis, [(i, i ^ 1) for i in range(length)])  2.92 us
  transfers between devices with their start and end apart: 5, of which 5 were waited for; matrix products, arithmetic and copies ran while one was open for 7% of the time, Pallas kernels for 0%

profile of v3, /device:TPU:64, one launch (start us, length us, event | category | flops | bytes accessed | tf_op | source)
XLA Modules:
  0.0 129.9 jit_solution(14871266719263387544)
XLA Ops:
  0.7 7.8 %collective-permute-start.1 = (bf16[1,64,3584]{2,1,0:T(8,128)(2,1)}, bf16[1,64,3584]{2,1,0:T(8,128)(2,1)S(1)}, u32[]{:S(2)}, u32[]{:S(2)}) collective-permute-start(bf16[1,64,3584]{2,1,0:T(8,128)(2,1)} %param.12), channel_id=1, source_target_pairs={{0,720},{48,0},{96,48},{144,96},{192,144},{240,192},{288,240},{336... | collective-permute-start | bytes 1376264 | tf_op jit(solution)/shard_map/ppermute | solution.py:14
  8.5 1.9 %collective-permute-start = (bf16[1,64,3584]{2,1,0:T(8,128)(2,1)}, bf16[1,64,3584]{2,1,0:T(8,128)(2,1)S(1)}, u32[]{:S(2)}, u32[]{:S(2)}) collective-permute-start(bf16[1,64,3584]{2,1,0:T(8,128)(2,1)} %param.10), channel_id=1, source_target_pairs={{0,48},{48,96},{96,144},{144,192},{192,240},{240,288},{288,336},{3... | collective-permute-start | bytes 1376264 | tf_op jit(solution)/shard_map/ppermute | solution.py:14
  10.4 1.5 %copy.25 = bf16[1,3584,128]{1,2,0:T(8,128)(2,1)S(1)} copy(bf16[1,3584,128]{2,1,0:T(8,128)(2,1)} %param.14) | data formatting | bytes 1835008 | tf_op args[4]
  11.9 2.2 %copy.24 = bf16[1,3584,128]{1,2,0:T(8,128)(2,1)} copy(bf16[1,3584,128]{2,1,0:T(8,128)(2,1)} %param.13) | data formatting | bytes 1835008 | tf_op args[3]
  14.3 2.9 %pad_maximum_fusion = bf16[384,3584]{1,0:T(8,128)(2,1)} fusion(bf16[128,3584]{1,0:T(8,128)(2,1)S(1)} %bitcast.62, bf16[128,3584]{1,0:T(8,128)(2,1)} %bitcast.63, bf16[128,3584]{1,0:T(8,128)(2,1)S(1)} %bitcast.61), kind=kLoop, calls=%fused_computation.5 | loop fusion | flops 8257536 | bytes 5505024 | tf_op jit(solution)/shard_map/concatenate | solution.py:110
  17.6 0.6 fusion.32
  18.9 7.6 %collective-permute-done = bf16[1,64,3584]{2,1,0:T(8,128)(2,1)S(1)} collective-permute-done((bf16[1,64,3584]{2,1,0:T(8,128)(2,1)}, bf16[1,64,3584]{2,1,0:T(8,128)(2,1)S(1)}, u32[]{:S(2)}, u32[]{:S(2)}) %collective-permute-start) | collective-permute-done | bytes 458784 | tf_op jit(solution)/shard_map/ppermute | solution.py:14
  27.1 46.5 %all_to_all.10 = bf16[24,4,3584]{2,1,0:T(4,128)(2,1)} all-to-all(bf16[24,4,3584]{2,1,0:T(4,128)(2,1)S(1)} %bitcast.64), channel_id=1, replica_groups={{0,2,4,6,8,10,12,14,16,18,20,22,24,26,28,30,32,34,36,38,40,42,44,46},{1..., dimensions={0} | all-to-all | bytes 1376256 | tf_op jit(solution)/shard_map/all_to_all | solution.py:120
  73.5 1.5 %reshape.53 = bf16[96,3584]{1,0:T(8,128)(2,1)S(1)} reshape(bf16[24,4,3584]{2,1,0:T(4,128)(2,1)} %all_to_all.10) | data formatting | bytes 1376256 | tf_op jit(solution)/shard_map/reshape | solution.py:121
  75.1 2.2 %collective-permute-start.2 = (bf16[96,3584]{1,0:T(8,128)(2,1)S(1)}, bf16[96,3584]{1,0:T(8,128)(2,1)S(1)}, u32[]{:S(2)}, u32[]{:S(2)}) collective-permute-start(bf16[96,3584]{1,0:T(8,128)(2,1)S(1)} %reshape.53), channel_id=1, source_target_pairs={{0,1},{1,0},{2,3},{3,2},{4,5},{5,4},{6,7},{7,6},{8,9},{9,8},{10,11... | collective-permute-start | bytes 2064392 | tf_op jit(solution)/shard_map/ppermute | solution.py:19
  77.3 2.1 %collective-permute-done.2 = bf16[96,3584]{1,0:T(8,128)(2,1)S(1)} collective-permute-done((bf16[96,3584]{1,0:T(8,128)(2,1)S(1)}, bf16[96,3584]{1,0:T(8,128)(2,1)S(1)}, u32[]{:S(2)}, u32[]{:S(2)}) %collective-permute-start.2) | collective-permute-done | bytes 688160 | tf_op jit(solution)/shard_map/ppermute | solution.py:19
  79.7 1.6 %multiply_convert_fusion.1 = (bf16[96,128]{1,0:T(8,128)(2,1)S(1)}, bf16[96,128]{1,0:T(8,128)(2,1)S(1)}) fusion(f32[96,128]{1,0:T(8,128)} %bitcast.68, f32[96,128]{1,0:T(8,128)} %bitcast.67, bf16[96,3584]{1,0:T(8,128)(2,1)S(1)} %collective-permute-done.2, bf16[1,128,3584]{2,1,0:T(8,128)(2,1)} %param.15), kind=kOutput, calls=%fused_computation.31 | convolution fusion | flops 88240128 | bytes 1753088 | tf_op jit(solution)/shard_map/dot_general | solution.py:127
  81.4 0.4 select_convert_fusion
  81.8 0.6 convolution_convert_fusion
  82.4 2.0 %collective-permute-start.3 = (bf16[96,3584]{1,0:T(8,128)(2,1)S(1)}, bf16[96,3584]{1,0:T(8,128)(2,1)S(1)}, u32[]{:S(2)}, u32[]{:S(2)}) collective-permute-start(bf16[96,3584]{1,0:T(8,128)(2,1)S(1)} %convolution_convert_fusion), channel_id=1, source_target_pairs={{0,1},{1,0},{2,3},{3,2},{4,5},{5,4},{6,7},{7,6},{8,9},{9,8},{10,11... | collective-permute-start | bytes 2064392 | tf_op jit(solution)/shard_map/ppermute | solution.py:19
  84.5 0.3 fusion.8
  84.8 0.4 fusion.2
  85.2 0.4 multiply_convert_fusion.3
  85.6 0.8 collective-permute-done.3
  86.5 0.7 add_convert_fusion
  87.1 1.0 reshape.54
  88.2 7.9 %all-to-all-start.1 = ((bf16[24,4,3584]{2,1,0:T(4,128)(2,1)}), bf16[24,4,3584]{2,1,0:T(4,128)(2,1)S(1)}, u32[]{:S(2)}, u32[]{:S(2)}) async-start(bf16[24,4,3584]{2,1,0:T(4,128)(2,1)} %reshape.54), calls=%async_computation.1 | async-start | bytes 1376256 | tf_op jit(solution)/shard_map/all_to_all | solution.py:140
  96.4 31.1 %all-to-all-done.1.back = bf16[24,4,3584]{2,1,0:T(4,128)(2,1)S(1)} async-done(((bf16[24,4,3584]{2,1,0:T(4,128)(2,1)}), bf16[24,4,3584]{2,1,0:T(4,128)(2,1)S(1)}, u32[]{:S(2)}, u32[]{:S(2)}) %all-to-all-start.1) | async-done | bytes 688160 | tf_op jit(solution)/shard_map/all_to_all | solution.py:140
  127.5 2.4 %settle.1 = (bf16[64,3584]{1,0:T(8,128)(2,1)}, bf16[64,3584]{1,0:T(8,128)(2,1)}) custom-call(s32[6]{0:T(128)S(1)} %reshape.46.fwd_slots, f32[6]{0:T(128)S(1)} %reshape.47.fwd_gates, s32[6]{0:T(128)S(1)} %reshape.48.bwd_slots, f32[6]{0:T(128)S(1)} %reshape.49.bwd_gates, bf16[24,4,3584]{2,1,0:T(4,128)(2,1)S(1)} %all-to-all-done.1.back, ...), custom_call_target="tpu_custom_call" | custom-call | flops 688128 | bytes 2293760 | tf_op jit(solution)/shard_map/settle/pallas_call | solution.py:59
  (43 shorter events, 2.4 us)
Async XLA Ops:
  0.6 13.5 %copy-start.5 = (bf16[1,48,2,2,128]{4,3,2,1,0:T(2,128)(2,1)S(1)}, bf16[1,48,2,2,128]{4,3,2,1,0:T(2,128)(2,1)}, u32[]{:S(2)}) copy-start(bf16[1,48,2,2,128]{4,3,2,1,0:T(2,128)(2,1)} %param.11) | copy-start | bytes 147460
  0.6 13.6 %copy-start.3 = (bf16[1,128,3584]{2,1,0:T(8,128)(2,1)S(1)}, bf16[1,128,3584]{2,1,0:T(8,128)(2,1)}, u32[]{:S(2)}) copy-start(bf16[1,128,3584]{2,1,0:T(8,128)(2,1)} %param.15) | copy-start | bytes 2752516
  0.7 17.9 %collective-permute-start.1 = (bf16[1,64,3584]{2,1,0:T(8,128)(2,1)}, bf16[1,64,3584]{2,1,0:T(8,128)(2,1)S(1)}, u32[]{:S(2)}, u32[]{:S(2)}) collective-permute-start(bf16[1,64,3584]{2,1,0:T(8,128)(2,1)} %param.12), channel_id=1, source_target_pairs={{0,720},{48,0},{96,48},{144,96},{192,144},{240,192},{288,240},{336... | collective-permute-start | bytes 1376264 | tf_op jit(solution)/shard_map/ppermute | solution.py:14
  8.5 18.0 %collective-permute-start = (bf16[1,64,3584]{2,1,0:T(8,128)(2,1)}, bf16[1,64,3584]{2,1,0:T(8,128)(2,1)S(1)}, u32[]{:S(2)}, u32[]{:S(2)}) collective-permute-start(bf16[1,64,3584]{2,1,0:T(8,128)(2,1)} %param.10), channel_id=1, source_target_pairs={{0,48},{48,96},{96,144},{144,192},{192,240},{240,288},{288,336},{3... | collective-permute-start | bytes 1376264 | tf_op jit(solution)/shard_map/ppermute | solution.py:14
  14.3 3.0 %copy-start.6 = (s32[1,1,3,2]{2,3,1,0:T(2,128)S(1)}, s32[1,1,3,2]{2,3,1,0:T(2,128)}, u32[]{:S(2)}) copy-start(s32[1,1,3,2]{2,3,1,0:T(2,128)} %param.16) | copy-start | bytes 76
  14.3 3.2 %copy-start.7 = (s32[1,1,3,2]{2,3,1,0:T(2,128)S(1)}, s32[1,1,3,2]{2,3,1,0:T(2,128)}, u32[]{:S(2)}) copy-start(s32[1,1,3,2]{2,3,1,0:T(2,128)} %param.18) | copy-start | bytes 76
  17.2 62.2 %copy-start.1 = (bf16[1,3584,128]{2,1,0:T(8,128)(2,1)S(1)}, bf16[1,3584,128]{2,1,0:T(8,128)(2,1)}, u32[]{:S(2)}) copy-start(bf16[1,3584,128]{2,1,0:T(8,128)(2,1)} %param.13) | copy-start | bytes 2752516
  27.1 54.3 %copy-start.2 = (bf16[1,3584,128]{2,1,0:T(8,128)(2,1)S(1)}, bf16[1,3584,128]{2,1,0:T(8,128)(2,1)}, u32[]{:S(2)}) copy-start(bf16[1,3584,128]{2,1,0:T(8,128)(2,1)} %param.14) | copy-start | bytes 2752516
  75.1 6.7 %copy-start = (bf16[384,3584]{1,0:T(8,128)(2,1)S(1)}, bf16[384,3584]{1,0:T(8,128)(2,1)}, u32[]{:S(2)}) copy-start(bf16[384,3584]{1,0:T(8,128)(2,1)} %pad_maximum_fusion) | copy-start | bytes 8257540
  75.1 4.3 %collective-permute-start.2 = (bf16[96,3584]{1,0:T(8,128)(2,1)S(1)}, bf16[96,3584]{1,0:T(8,128)(2,1)S(1)}, u32[]{:S(2)}, u32[]{:S(2)}) collective-permute-start(bf16[96,3584]{1,0:T(8,128)(2,1)S(1)} %reshape.53), channel_id=1, source_target_pairs={{0,1},{1,0},{2,3},{3,2},{4,5},{5,4},{6,7},{7,6},{8,9},{9,8},{10,11... | collective-permute-start | bytes 2064392 | tf_op jit(solution)/shard_map/ppermute | solution.py:19
  81.8 3.4 %copy-start.4 = (bf16[1,128,3584]{2,1,0:T(8,128)(2,1)S(1)}, bf16[1,128,3584]{2,1,0:T(8,128)(2,1)}, u32[]{:S(2)}) copy-start(bf16[1,128,3584]{2,1,0:T(8,128)(2,1)} %param.15) | copy-start | bytes 2752516
  82.4 4.0 %collective-permute-start.3 = (bf16[96,3584]{1,0:T(8,128)(2,1)S(1)}, bf16[96,3584]{1,0:T(8,128)(2,1)S(1)}, u32[]{:S(2)}, u32[]{:S(2)}) collective-permute-start(bf16[96,3584]{1,0:T(8,128)(2,1)S(1)} %convolution_convert_fusion), channel_id=1, source_target_pairs={{0,1},{1,0},{2,3},{3,2},{4,5},{5,4},{6,7},{7,6},{8,9},{9,8},{10,11... | collective-permute-start | bytes 2064392 | tf_op jit(solution)/shard_map/ppermute | solution.py:19
  86.5 9.6 %copy-start.8 = (f32[1,1,3,2]{2,3,1,0:T(2,128)S(1)}, f32[1,1,3,2]{2,3,1,0:T(2,128)}, u32[]{:S(2)}) copy-start(f32[1,1,3,2]{2,3,1,0:T(2,128)} %param.17) | copy-start | bytes 76
  86.5 9.8 %copy-start.9 = (f32[1,1,3,2]{2,3,1,0:T(2,128)S(1)}, f32[1,1,3,2]{2,3,1,0:T(2,128)}, u32[]{:S(2)}) copy-start(f32[1,1,3,2]{2,3,1,0:T(2,128)} %param.19) | copy-start | bytes 76
  88.2 39.4 %all-to-all-start.1 = ((bf16[24,4,3584]{2,1,0:T(4,128)(2,1)}), bf16[24,4,3584]{2,1,0:T(4,128)(2,1)S(1)}, u32[]{:S(2)}, u32[]{:S(2)}) async-start(bf16[24,4,3584]{2,1,0:T(4,128)(2,1)} %reshape.54), calls=%async_computation.1 | async-start | bytes 1376256 | tf_op jit(solution)/shard_map/all_to_all | solution.py:140

commit v4 on v3

--- a/solution.py
+++ b/solution.py
@@ -98,17 +98,6 @@
     fwd_index = fwd_slots.reshape(-1)
     bwd_index = bwd_slots.reshape(-1)
 
-    saved = saved_preact[0].reshape(chips, CORES, cap, 2, hidden_width)
-
-    def saved_of(which):
-        part = lax.dynamic_index_in_dim(saved, which, 1, keepdims=False)
-        part = jnp.concatenate([jnp.zeros_like(part), part], axis=1)
-        part = part.transpose(2, 0, 1, 3).reshape(2, -1, hidden_width).astype(jnp.float32)
-        return part[0], part[1]
-
-    saves = (*saved_of(core), *saved_of(1 - core))
-    w_out = jnp.concatenate([w_down, w_gate.T, w_up.T], axis=0)
-
     fwd_rows = pick_rows(fwd_index, inputs)
     bwd_rows = pick_rows(bwd_index, incoming)
     rows = jnp.concatenate(
@@ -116,27 +105,32 @@
     )
     rows = jnp.broadcast_to(rows[:, None], (GROUPS, chips // GROUPS, both, width))
     rows = rows.reshape(chips, both, width)
-    rows, w_out, saves = lax.optimization_barrier((rows, w_out, saves))
+    rows, w_gate, w_up, saved = lax.optimization_barrier((rows, w_gate, w_up, saved_preact[0]))
     rows = lax.all_to_all(rows, "expert", 0, 0, axis_index_groups=same_core, tiled=True)
-    mine = rows.reshape(chips * both, width)
-    other = swapped(mine, "expert")
+    rows = rows.reshape(chips * both, width)
 
-    def expert(rows, pre_a, pre_v):
-        pre_gate = jnp.dot(rows, w_gate, preferred_element_type=jnp.float32)
-        pre_up = jnp.dot(rows, w_up, preferred_element_type=jnp.float32)
-        dh = lax.dot_general(rows, w_down, (((1,), (1,)), ((), ())), preferred_element_type=jnp.float32)
+    own = jnp.concatenate([w_down, w_gate.T, w_up.T], axis=0)
+    other = swapped(own, "expert")
+    saved = saved.reshape(chips, CORES, cap, 2, hidden_width)
+    own_saved = lax.dynamic_index_in_dim(saved, core, 1, keepdims=False)
+    other_saved = swapped(lax.dynamic_index_in_dim(saved, 1 - core, 1, keepdims=False), "expert")
+
+    def acts_of(weights, saved):
+        pre = lax.dot_general(rows, weights, (((1,), (1,)), ((), ())), preferred_element_type=jnp.float32)
+        dh, pre_gate, pre_up = jnp.split(pre, 3, axis=1)
+        saved = jnp.concatenate([jnp.zeros_like(saved), saved], axis=1)
+        saved = saved.transpose(2, 0, 1, 3).reshape(2, -1, hidden_width).astype(jnp.float32)
+        pre_a, pre_v = saved[0], saved[1]
         is_fwd = (lax.broadcasted_iota(jnp.int32, pre_gate.shape, 0) % both) < cap
         hidden = jnp.where(is_fwd, jax.nn.silu(pre_gate) * pre_up, 0.0)
         sig = jax.nn.sigmoid(pre_a)
         act = pre_a * sig
         slope = sig * (1.0 + pre_a * (1.0 - sig))
-        acts = jnp.concatenate([hidden, dh * pre_v * slope, dh * act], axis=1).astype(jnp.bfloat16)
-        return jnp.dot(acts, w_out, preferred_element_type=jnp.float32).astype(jnp.bfloat16)
+        return jnp.concatenate([hidden, dh * pre_v * slope, dh * act], axis=1).astype(jnp.bfloat16)
 
-    away = swapped(expert(other, *saves[2:]), "expert")
-    home = expert(mine, *saves[:2])
-    part = (home.astype(jnp.float32) + away.astype(jnp.float32)).astype(jnp.bfloat16)
-    part = part.reshape(chips, both, width)
+    part = jnp.dot(acts_of(own, own_saved), own, preferred_element_type=jnp.float32)
+    part = part + jnp.dot(acts_of(other, other_saved), other, preferred_element_type=jnp.float32)
+    part = part.astype(jnp.bfloat16).reshape(chips, both, width)
     part = lax.all_to_all(part, "expert", 0, 0, axis_index_groups=same_core, tiled=True)
     fwd_out, grad_out = settle(
         part, fwd_index, fwd_gates.reshape(-1), inputs, bwd_index, bwd_gates.reshape(-1), incoming

time: 130 us -> 126 us (0.969)
  the two profiles are of different devices: /device:TPU:64 before, /device:TPU:30 now
where the time goes in v4:
time: 126 us; the launch traced here: 125 us
  waiting for transfers between devices  60.7 us (48%)
  starting transfers between devices  38.4 us (30%)
  matrix products  10.8 us (9%)
  local copies, waits for them, and re-layouts  8.78 us (7%)
  other arithmetic  3.29 us (3%)
  Pallas kernels  2.4 us (2%)
    all_to_all x1, waiting for transfers between devices, local(): lax.all_to_all(part, 'expert', 0, 0, axis_index_groups=same_core, tiled=T...  29.6 us
    all_to_all x1, waiting for transfers between devices, local(): lax.all_to_all(rows, 'expert', 0, 0, axis_index_groups=same_core, tiled=T...  21 us
    all_to_all x1, starting transfers between devices, local(): lax.all_to_all(rows, 'expert', 0, 0, axis_index_groups=same_core, tiled=T...  15.2 us
    ppermute x2, starting transfers between devices, shifted(): lax.ppermute(shard, axis, [(i, (i + by) % length) for i in range(length)])  13 us
    ppermute x2, waiting for transfers between devices, shifted(): lax.ppermute(shard, axis, [(i, (i + by) % length) for i in range(length)])  7.64 us
    all_to_all x1, starting transfers between devices, local(): lax.all_to_all(part, 'expert', 0, 0, axis_index_groups=same_core, tiled=T...  5.87 us
    dot_general x2, matrix products, acts_of(): lax.dot_general(rows, weights, (((1,), (1,)), ((), ())), preferred_elemen...  5.49 us
    unnamed x12, local copies, waits for them, and re-layouts  4.65 us
  transfers between devices with their start and end apart: 6, of which 4 were waited for; matrix products, arithmetic and copies ran while one was open for 12% of the time, Pallas kernels for 0%

profile of v4, /device:TPU:30, one launch (start us, length us, event | category | flops | bytes accessed | tf_op | source)
XLA Modules:
  0.0 125.3 jit_solution(17769240827130179214)
XLA Ops:
  0.6 11.1 %collective-permute-start = (bf16[1,64,3584]{2,1,0:T(8,128)(2,1)}, bf16[1,64,3584]{2,1,0:T(8,128)(2,1)S(1)}, u32[]{:S(2)}, u32[]{:S(2)}) collective-permute-start(bf16[1,64,3584]{2,1,0:T(8,128)(2,1)} %param.10), channel_id=1, source_target_pairs={{0,48},{48,96},{96,144},{144,192},{192,240},{240,288},{288,336},{3... | collective-permute-start | bytes 1376264 | tf_op jit(solution)/shard_map/ppermute | solution.py:14
  11.7 1.9 %collective-permute-start.1 = (bf16[1,64,3584]{2,1,0:T(8,128)(2,1)}, bf16[1,64,3584]{2,1,0:T(8,128)(2,1)S(1)}, u32[]{:S(2)}, u32[]{:S(2)}) collective-permute-start(bf16[1,64,3584]{2,1,0:T(8,128)(2,1)} %param.12), channel_id=1, source_target_pairs={{0,720},{48,0},{96,48},{144,96},{192,144},{240,192},{288,240},{336... | collective-permute-start | bytes 1376264 | tf_op jit(solution)/shard_map/ppermute | solution.py:14
  13.6 0.8 copy.20
  14.5 0.8 copy.22
  15.3 1.5 %copy.24 = bf16[1,3584,128]{1,2,0:T(8,128)(2,1)S(1)} copy(bf16[1,3584,128]{2,1,0:T(8,128)(2,1)} %param.13) | data formatting | bytes 1835008 | tf_op args[3]
  16.8 1.5 %copy.25 = bf16[1,3584,128]{1,2,0:T(8,128)(2,1)S(1)} copy(bf16[1,3584,128]{2,1,0:T(8,128)(2,1)} %param.14) | data formatting | bytes 1835008 | tf_op args[4]
  18.3 0.2 convolution_convert_fusion.1
  18.5 7.6 %collective-permute-done.1 = bf16[1,64,3584]{2,1,0:T(8,128)(2,1)S(1)} collective-permute-done((bf16[1,64,3584]{2,1,0:T(8,128)(2,1)}, bf16[1,64,3584]{2,1,0:T(8,128)(2,1)S(1)}, u32[]{:S(2)}, u32[]{:S(2)}) %collective-permute-start.1) | collective-permute-done | bytes 458784 | tf_op jit(solution)/shard_map/ppermute | solution.py:14
  26.6 1.0 broadcast_in_dim.19
  27.6 15.2 %all-to-all-start = ((bf16[24,4,3584]{2,1,0:T(4,128)(2,1)}), bf16[24,4,3584]{2,1,0:T(4,128)(2,1)}, u32[]{:S(2)}, u32[]{:S(2)}) async-start(bf16[24,4,3584]{2,1,0:T(4,128)(2,1)} %bitcast.2), calls=%async_computation | async-start | bytes 1376256 | tf_op jit(solution)/shard_map/all_to_all | solution.py:109
  42.8 2.9 %pad_maximum_fusion = bf16[384,3584]{1,0:T(8,128)(2,1)} fusion(bf16[128,3584]{1,0:T(8,128)(2,1)S(1)} %bitcast.39, bf16[128,3584]{1,0:T(8,128)(2,1)S(1)} %bitcast.38, bf16[128,3584]{1,0:T(8,128)(2,1)} %bitcast.40), kind=kLoop, calls=%fused_computation.4 | loop fusion | flops 8257536 | bytes 5505024 | tf_op jit(solution)/shard_map/concatenate | solution.py:112
  45.7 1.9 %collective-permute-start.2 = (bf16[384,3584]{1,0:T(8,128)(2,1)}, bf16[384,3584]{1,0:T(8,128)(2,1)}, u32[]{:S(2)}, u32[]{:S(2)}) collective-permute-start(bf16[384,3584]{1,0:T(8,128)(2,1)} %pad_maximum_fusion), channel_id=1, source_target_pairs={{0,1},{1,0},{2,3},{3,2},{4,5},{5,4},{6,7},{7,6},{8,9},{9,8},{10,11... | collective-permute-start | bytes 8257544 | tf_op jit(solution)/shard_map/ppermute | solution.py:19
  47.8 2.4 %collective-permute-start.3 = (bf16[24,2,2,128]{3,1,0,2:T(2,128)(2,1)S(1)}, bf16[24,2,2,128]{3,1,0,2:T(2,128)(2,1)S(1)}, u32[]{:S(2)}, u32[]{:S(2)}) collective-permute-start(bf16[24,2,2,128]{3,1,0,2:T(2,128)(2,1)S(1)} %bitcast.47), channel_id=1, source_target_pairs={{0,1},{1,0},{2,3},{3,2},{4,5},{5,4},{6,7},{7,6},{8,9},{9,8},{10,11... | collective-permute-start | bytes 73736 | tf_op jit(solution)/shard_map/ppermute | solution.py:19
  50.3 2.5 %collective-permute-done.3 = bf16[24,2,2,128]{3,1,0,2:T(2,128)(2,1)S(1)} collective-permute-done((bf16[24,2,2,128]{3,1,0,2:T(2,128)(2,1)S(1)}, bf16[24,2,2,128]{3,1,0,2:T(2,128)(2,1)S(1)}, u32[]{:S(2)}, u32[]{:S(2)}) %collective-permute-start.3) | collective-permute-done | bytes 24608 | tf_op jit(solution)/shard_map/ppermute | solution.py:19
  52.8 21.0 %all-to-all-done = bf16[24,4,3584]{2,1,0:T(4,128)(2,1)} async-done(((bf16[24,4,3584]{2,1,0:T(4,128)(2,1)}), bf16[24,4,3584]{2,1,0:T(4,128)(2,1)}, u32[]{:S(2)}, u32[]{:S(2)}) %all-to-all-start) | async-done | bytes 688160 | tf_op jit(solution)/shard_map/all_to_all | solution.py:109
  73.9 1.5 %reshape.56 = bf16[96,3584]{1,0:T(8,128)(2,1)S(1)} reshape(bf16[24,4,3584]{2,1,0:T(4,128)(2,1)} %all-to-all-done) | data formatting | bytes 1376256 | tf_op jit(solution)/shard_map/reshape | solution.py:110
  75.4 2.7 %fusion.24 = f32[96,384]{1,0:T(8,128)S(1)} fusion(bf16[96,3584]{1,0:T(8,128)(2,1)S(1)} %reshape.56, bf16[384,3584]{1,0:T(8,128)(2,1)} %pad_maximum_fusion), kind=kOutput, calls=%fused_computation.49 | convolution fusion | flops 264241152 | bytes 3588096 | tf_op jit(solution)/shard_map/dot_general | solution.py:119
  78.2 2.4 %fusion.1 = f32[96,3584]{1,0:T(8,128)S(1)} fusion(bf16[384,3584]{1,0:T(8,128)(2,1)} %pad_maximum_fusion, bf16[96,128]{1,0:T(8,128)(2,1)S(1)} %get-tuple-element.17, bf16[96,128]{1,0:T(8,128)(2,1)S(1)} %get-tuple-element.16, bf16[96,128]{1,0:T(8,128)(2,1)S(1)} %get-tuple-element.19), kind=kOutput, calls=%fused_computation.8 | convolution fusion | flops 264462336 | bytes 4202496 | tf_op jit(solution)/shard_map/dot_general | solution.py:131
  80.7 2.7 %fusion.25 = f32[96,384]{1,0:T(8,128)S(1)} fusion(bf16[96,3584]{1,0:T(8,128)(2,1)S(1)} %reshape.56, bf16[384,3584]{1,0:T(8,128)(2,1)} %collective-permute-done.2), kind=kOutput, calls=%fused_computation.50 | convolution fusion | flops 264241152 | bytes 3588096 | tf_op jit(solution)/shard_map/dot_general | solution.py:119
  83.6 2.5 %fusion = bf16[96,3584]{1,0:T(8,128)(2,1)S(1)} fusion(f32[96,3584]{1,0:T(8,128)S(1)} %fusion.1, bf16[384,3584]{1,0:T(8,128)(2,1)} %collective-permute-done.2, bf16[96,128]{1,0:T(8,128)(2,1)S(1)} %get-tuple-element.15, bf16[96,128]{1,0:T(8,128)(2,1)S(1)} %get-tuple-element.14, bf16[96,128]{1,0:T(8,128)(2,1)S(1)} %get-tuple-element.18), kind=kOutput, calls=%fused_computation.1 | convolution fusion | flops 265150464 | bytes 4890624 | tf_op jit(solution)/shard_map/dot_general | solution.py:132
  86.0 1.0 reshape.58
  87.1 5.9 %all-to-all-start.1 = ((bf16[24,4,3584]{2,1,0:T(4,128)(2,1)}), bf16[24,4,3584]{2,1,0:T(4,128)(2,1)S(1)}, u32[]{:S(2)}, u32[]{:S(2)}) async-start(bf16[24,4,3584]{2,1,0:T(4,128)(2,1)} %reshape.58), calls=%async_computation.1 | async-start | bytes 1376256 | tf_op jit(solution)/shard_map/all_to_all | solution.py:134
  93.3 29.6 %all-to-all-done.1.back = bf16[24,4,3584]{2,1,0:T(4,128)(2,1)S(1)} async-done(((bf16[24,4,3584]{2,1,0:T(4,128)(2,1)}), bf16[24,4,3584]{2,1,0:T(4,128)(2,1)S(1)}, u32[]{:S(2)}, u32[]{:S(2)}) %all-to-all-start.1) | async-done | bytes 688160 | tf_op jit(solution)/shard_map/all_to_all | solution.py:134
  122.9 2.4 %settle.1 = (bf16[64,3584]{1,0:T(8,128)(2,1)}, bf16[64,3584]{1,0:T(8,128)(2,1)}) custom-call(s32[6]{0:T(128)S(1)} %reshape.49.fwd_slots, f32[6]{0:T(128)S(1)} %reshape.50.fwd_gates, s32[6]{0:T(128)S(1)} %reshape.51.bwd_slots, f32[6]{0:T(128)S(1)} %reshape.52.bwd_gates, bf16[24,4,3584]{2,1,0:T(4,128)(2,1)S(1)} %all-to-all-done.1.back, ...), custom_call_target="tpu_custom_call" | custom-call | flops 688128 | bytes 2293760 | tf_op jit(solution)/shard_map/settle/pallas_call | solution.py:59
  (29 shorter events, 1.4 us)
Async XLA Ops:
  0.6 17.6 %collective-permute-start = (bf16[1,64,3584]{2,1,0:T(8,128)(2,1)}, bf16[1,64,3584]{2,1,0:T(8,128)(2,1)S(1)}, u32[]{:S(2)}, u32[]{:S(2)}) collective-permute-start(bf16[1,64,3584]{2,1,0:T(8,128)(2,1)} %param.10), channel_id=1, source_target_pairs={{0,48},{48,96},{96,144},{144,192},{192,240},{240,288},{288,336},{3... | collective-permute-start | bytes 1376264 | tf_op jit(solution)/shard_map/ppermute | solution.py:14
  11.7 14.5 %collective-permute-start.1 = (bf16[1,64,3584]{2,1,0:T(8,128)(2,1)}, bf16[1,64,3584]{2,1,0:T(8,128)(2,1)S(1)}, u32[]{:S(2)}, u32[]{:S(2)}) collective-permute-start(bf16[1,64,3584]{2,1,0:T(8,128)(2,1)} %param.12), channel_id=1, source_target_pairs={{0,720},{48,0},{96,48},{144,96},{192,144},{240,192},{288,240},{336... | collective-permute-start | bytes 1376264 | tf_op jit(solution)/shard_map/ppermute | solution.py:14
  27.6 46.2 %all-to-all-start = ((bf16[24,4,3584]{2,1,0:T(4,128)(2,1)}), bf16[24,4,3584]{2,1,0:T(4,128)(2,1)}, u32[]{:S(2)}, u32[]{:S(2)}) async-start(bf16[24,4,3584]{2,1,0:T(4,128)(2,1)} %bitcast.2), calls=%async_computation | async-start | bytes 1376256 | tf_op jit(solution)/shard_map/all_to_all | solution.py:109
  42.8 4.9 %copy-start = (bf16[1,48,2,2,128]{4,3,2,1,0:T(2,128)(2,1)S(1)}, bf16[1,48,2,2,128]{4,3,2,1,0:T(2,128)(2,1)}, u32[]{:S(2)}) copy-start(bf16[1,48,2,2,128]{4,3,2,1,0:T(2,128)(2,1)} %param.11) | copy-start | bytes 147460
  45.7 34.9 %collective-permute-start.2 = (bf16[384,3584]{1,0:T(8,128)(2,1)}, bf16[384,3584]{1,0:T(8,128)(2,1)}, u32[]{:S(2)}, u32[]{:S(2)}) collective-permute-start(bf16[384,3584]{1,0:T(8,128)(2,1)} %pad_maximum_fusion), channel_id=1, source_target_pairs={{0,1},{1,0},{2,3},{3,2},{4,5},{5,4},{6,7},{7,6},{8,9},{9,8},{10,11... | collective-permute-start | bytes 8257544 | tf_op jit(solution)/shard_map/ppermute | solution.py:19
  47.8 5.0 %collective-permute-start.3 = (bf16[24,2,2,128]{3,1,0,2:T(2,128)(2,1)S(1)}, bf16[24,2,2,128]{3,1,0,2:T(2,128)(2,1)S(1)}, u32[]{:S(2)}, u32[]{:S(2)}) collective-permute-start(bf16[24,2,2,128]{3,1,0,2:T(2,128)(2,1)S(1)} %bitcast.47), channel_id=1, source_target_pairs={{0,1},{1,0},{2,3},{3,2},{4,5},{5,4},{6,7},{7,6},{8,9},{9,8},{10,11... | collective-permute-start | bytes 73736 | tf_op jit(solution)/shard_map/ppermute | solution.py:19
  83.6 9.4 %copy-start.1 = (f32[1,1,3,2]{2,3,1,0:T(2,128)S(1)}, f32[1,1,3,2]{2,3,1,0:T(2,128)}, u32[]{:S(2)}) copy-start(f32[1,1,3,2]{2,3,1,0:T(2,128)} %param.17) | copy-start | bytes 76
  83.6 9.6 %copy-start.2 = (f32[1,1,3,2]{2,3,1,0:T(2,128)S(1)}, f32[1,1,3,2]{2,3,1,0:T(2,128)}, u32[]{:S(2)}) copy-start(f32[1,1,3,2]{2,3,1,0:T(2,128)} %param.19) | copy-start | bytes 76
  87.1 35.8 %all-to-all-start.1 = ((bf16[24,4,3584]{2,1,0:T(4,128)(2,1)}), bf16[24,4,3584]{2,1,0:T(4,128)(2,1)S(1)}, u32[]{:S(2)}, u32[]{:S(2)}) async-start(bf16[24,4,3584]{2,1,0:T(4,128)(2,1)} %reshape.58), calls=%async_computation.1 | async-start | bytes 1376256 | tf_op jit(solution)/shard_map/all_to_all | solution.py:134

commit v5 on v4

--- a/solution.py
+++ b/solution.py
@@ -67,6 +67,82 @@
         cost_estimate=pl.CostEstimate(flops=2 * chips * both * width, bytes_accessed=2560 * width // 4, transcendentals=0),
         name="settle",
     )(fwd_slots, fwd_gates, bwd_slots, bwd_gates, back, inputs, incoming)
+
+
+def expert_kernel(rows, own, other, own_saved, other_saved, out, rows_in, lhs, weights, rows_sem, sems):
+    chips, both, width = rows.shape
+    count, piece = own_saved.shape[1:]
+    parts = sems.shape[1]
+    step = width // parts
+    columns = [pl.ds(part * step, step) for part in range(parts)]
+    rows_copy = pltpu.make_async_copy(rows, rows_in, rows_sem)
+    rows_copy.start()
+    copies = []
+    for part in range(parts):
+        for which, source in enumerate((own, other)):
+            copy = pltpu.make_async_copy(
+                source.at[:, columns[part]], weights.at[which, :, columns[part]], sems.at[which, part]
+            )
+            copy.start()
+            copies.append(copy)
+    rows_copy.wait()
+    for chip in range(chips):
+        lhs[pl.ds(chip * both, both)] = rows_in[chip].astype(jnp.float32)
+    pre = [jnp.zeros((count, 3 * piece), jnp.float32) for _ in range(2)]
+    for part in range(parts):
+        left = lhs[:, columns[part]].astype(jnp.bfloat16)
+        for which in range(2):
+            copies[2 * part + which].wait()
+            pre[which] = pre[which] + lax.dot_general(
+                left,
+                weights[which, :, columns[part]],
+                (((1,), (1,)), ((), ())),
+                preferred_element_type=jnp.float32,
+            )
+    is_fwd = lax.rem(lax.broadcasted_iota(jnp.int32, (count, piece), 0), both) < both // 2
+    acts = []
+    for which, saved in enumerate((own_saved, other_saved)):
+        dh = pre[which][:, :piece]
+        pre_gate = pre[which][:, piece : 2 * piece]
+        pre_up = pre[which][:, 2 * piece :]
+        hidden = jnp.where(is_fwd, jax.nn.silu(pre_gate) * pre_up, 0.0)
+        pre_a = saved[0]
+        pre_v = saved[1]
+        sig = jax.nn.sigmoid(pre_a)
+        slope = sig * (1.0 + pre_a * (1.0 - sig))
+        d_gate = dh * pre_v * slope
+        d_up = dh * (pre_a * sig)
+        acts.append(jnp.concatenate([hidden, d_gate, d_up], axis=1).astype(jnp.bfloat16))
+    for part in range(parts):
+        total = jnp.dot(acts[0], weights[0, :, columns[part]], preferred_element_type=jnp.float32)
+        total = total + jnp.dot(acts[1], weights[1, :, columns[part]], preferred_element_type=jnp.float32)
+        for chip in range(chips):
+            out[chip, :, columns[part]] = total[chip * both : (chip + 1) * both].astype(out.dtype)
+
+
+def expert(rows, own, other, own_saved, other_saved):
+    chips, both, width = rows.shape
+    parts = 4
+    vmem = pl.BlockSpec(memory_space=pltpu.VMEM)
+    anywhere = pl.BlockSpec(memory_space=pl.ANY)
+    return pl.pallas_call(
+        expert_kernel,
+        out_shape=jax.ShapeDtypeStruct(rows.shape, jnp.bfloat16),
+        in_specs=[anywhere] * 3 + [vmem] * 2,
+        out_specs=vmem,
+        scratch_shapes=[
+            pltpu.VMEM(rows.shape, jnp.bfloat16),
+            pltpu.VMEM((chips * both, width), jnp.float32),
+            pltpu.VMEM((2, *own.shape), jnp.bfloat16),
+            pltpu.SemaphoreType.DMA,
+            pltpu.SemaphoreType.DMA((2, parts)),
+        ],
+        compiler_params=pltpu.CompilerParams(vmem_limit_bytes=24 * 1024 * 1024),
+        cost_estimate=pl.CostEstimate(
+            flops=8 * chips * both * own.size, bytes_accessed=4 * own.size, transcendentals=0
+        ),
+        name="expert",
+    )(rows, own, other, own_saved, other_saved)
 
 
 def local(
@@ -107,7 +183,6 @@
     rows = rows.reshape(chips, both, width)
     rows, w_gate, w_up, saved = lax.optimization_barrier((rows, w_gate, w_up, saved_preact[0]))
     rows = lax.all_to_all(rows, "expert", 0, 0, axis_index_groups=same_core, tiled=True)
-    rows = rows.reshape(chips * both, width)
 
     own = jnp.concatenate([w_down, w_gate.T, w_up.T], axis=0)
     other = swapped(own, "expert")
@@ -115,22 +190,11 @@
     own_saved = lax.dynamic_index_in_dim(saved, core, 1, keepdims=False)
     other_saved = swapped(lax.dynamic_index_in_dim(saved, 1 - core, 1, keepdims=False), "expert")
 
-    def acts_of(weights, saved):
-        pre = lax.dot_general(rows, weights, (((1,), (1,)), ((), ())), preferred_element_type=jnp.float32)
-        dh, pre_gate, pre_up = jnp.split(pre, 3, axis=1)
+    def in_row_order(saved):
         saved = jnp.concatenate([jnp.zeros_like(saved), saved], axis=1)
-        saved = saved.transpose(2, 0, 1, 3).reshape(2, -1, hidden_width).astype(jnp.float32)
-        pre_a, pre_v = saved[0], saved[1]
-        is_fwd = (lax.broadcasted_iota(jnp.int32, pre_gate.shape, 0) % both) < cap
-        hidden = jnp.where(is_fwd, jax.nn.silu(pre_gate) * pre_up, 0.0)
-        sig = jax.nn.sigmoid(pre_a)
-        act = pre_a * sig
-        slope = sig * (1.0 + pre_a * (1.0 - sig))
-        return jnp.concatenate([hidden, dh * pre_v * slope, dh * act], axis=1).astype(jnp.bfloat16)
-
-    part = jnp.dot(acts_of(own, own_saved), own, preferred_element_type=jnp.float32)
-    part = part + jnp.dot(acts_of(other, other_saved), other, preferred_element_type=jnp.float32)
-    part = part.astype(jnp.bfloat16).reshape(chips, both, width)
+        return saved.transpose(2, 0, 1, 3).reshape(2, -1, hidden_width).astype(jnp.float32)
+
+    part = expert(rows, own, other, in_row_order(own_saved), in_row_order(other_saved))
     part = lax.all_to_all(part, "expert", 0, 0, axis_index_groups=same_core, tiled=True)
     fwd_out, grad_out = settle(
         part, fwd_index, fwd_gates.reshape(-1), inputs, bwd_index, bwd_gates.reshape(-1), incoming

time: 126 us -> 129 us (1.024)
  matrix products: 10.8 us -> 0.44 us
  waiting for transfers between devices: 60.7 us -> 66.5 us
  Pallas kernels: 2.4 us -> 7.54 us
  local copies, waits for them, and re-layouts: 8.78 us -> 11.5 us
    dot_general x4 -> x0, matrix products: 10.4 us -> none  [the longest x2 5.49 us: acts_of(): lax.dot_general(rows, weights, (((1,), (1,)), ((), ())), preferred_elemen...]
    all_to_all x1, waiting for transfers between devices: 21 us -> 28.1 us  [local(): lax.all_to_all(rows, 'expert', 0, 0, axis_index_groups=same_core, tiled=T...]
    unnamed x12 -> x24, local copies, waits for them, and re-layouts: 4.65 us -> 9.98 us
    pallas_call x0 -> x1, Pallas kernels: none -> 5.13 us  [expert(): pl.pallas_call(expert_kernel, out_shape=jax.ShapeDtypeStruct(rows.shape,...]
    reshape x2 -> x0, local copies, waits for them, and re-layouts: 2.54 us -> none  [the longest x1 1.52 us: local(): rows = rows.reshape(chips * both, width)]
    all_to_all x1, waiting for transfers between devices: 29.6 us -> 31.4 us  [local(): lax.all_to_all(part, 'expert', 0, 0, axis_index_groups=same_core, tiled=T...]
    ppermute x2, waiting for transfers between devices: 2.46 us -> 0.92 us  [swapped(): return lax.ppermute(shard, axis, [(i, i ^ 1) for i in range(length)])]
    ppermute x2, waiting for transfers between devices: 7.64 us -> 6.1 us  [shifted(): lax.ppermute(shard, axis, [(i, (i + by) % length) for i in range(length)])]
  transfers between devices with their start and end apart: 6 -> 6, of which waited for: 4 -> 4; matrix products, arithmetic and copies ran while one was open for 12% -> 6% of each run, Pallas kernels for 0% -> 0%
where the time goes in v5:
time: 129 us; the launch traced here: 128 us
  waiting for transfers between devices  66.5 us (52%)
  starting transfers between devices  38.9 us (30%)
  local copies, waits for them, and re-layouts  11.5 us (9%)
  Pallas kernels  7.54 us (6%)
  other arithmetic  2.71 us (2%)
    all_to_all x1, waiting for transfers between devices, local(): lax.all_to_all(part, 'expert', 0, 0, axis_index_groups=same_core, tiled=T...  31.4 us
    all_to_all x1, waiting for transfers between devices, local(): lax.all_to_all(rows, 'expert', 0, 0, axis_index_groups=same_core, tiled=T...  28.1 us
    all_to_all x1, starting transfers between devices, local(): lax.all_to_all(rows, 'expert', 0, 0, axis_index_groups=same_core, tiled=T...  15.1 us
    ppermute x2, starting transfers between devices, shifted(): lax.ppermute(shard, axis, [(i, (i + by) % length) for i in range(length)])  13 us
    unnamed x24, local copies, waits for them, and re-layouts  9.98 us
    all_to_all x1, starting transfers between devices, local(): lax.all_to_all(part, 'expert', 0, 0, axis_index_groups=same_core, tiled=T...  6.76 us
    ppermute x2, waiting for transfers between devices, shifted(): lax.ppermute(shard, axis, [(i, (i + by) % length) for i in range(length)])  6.1 us
    pallas_call x1, Pallas kernels, expert(): pl.pallas_call(expert_kernel, out_shape=jax.ShapeDtypeStruct(rows.shape,...  5.13 us
  transfers between devices with their start and end apart: 6, of which 4 were waited for; matrix products, arithmetic and copies ran while one was open for 6% of the time, Pallas kernels for 0%

profile of v5, /device:TPU:30, one launch (start us, length us, event | category | flops | bytes accessed | tf_op | source)
XLA Modules:
  0.0 128.5 jit_solution(8495465012076054077)
XLA Ops:
  0.6 11.1 %collective-permute-start = (bf16[1,64,3584]{2,1,0:T(8,128)(2,1)}, bf16[1,64,3584]{2,1,0:T(8,128)(2,1)S(1)}, u32[]{:S(2)}, u32[]{:S(2)}) collective-permute-start(bf16[1,64,3584]{2,1,0:T(8,128)(2,1)} %param.10), channel_id=1, source_target_pairs={{0,48},{48,96},{96,144},{144,192},{192,240},{240,288},{288,336},{3... | collective-permute-start | bytes 1376264 | tf_op jit(solution)/shard_map/ppermute | solution.py:14
  11.7 1.9 %collective-permute-start.1 = (bf16[1,64,3584]{2,1,0:T(8,128)(2,1)}, bf16[1,64,3584]{2,1,0:T(8,128)(2,1)S(1)}, u32[]{:S(2)}, u32[]{:S(2)}) collective-permute-start(bf16[1,64,3584]{2,1,0:T(8,128)(2,1)} %param.12), channel_id=1, source_target_pairs={{0,720},{48,0},{96,48},{144,96},{192,144},{240,192},{288,240},{336... | collective-permute-start | bytes 1376264 | tf_op jit(solution)/shard_map/ppermute | solution.py:14
  13.6 0.8 copy.20
  14.5 0.8 copy.22
  15.3 2.3 %copy.24 = bf16[1,3584,128]{1,2,0:T(8,128)(2,1)} copy(bf16[1,3584,128]{2,1,0:T(8,128)(2,1)} %param.13) | data formatting | bytes 1835008 | tf_op args[3]
  17.6 2.2 %copy.25 = bf16[1,3584,128]{1,2,0:T(8,128)(2,1)} copy(bf16[1,3584,128]{2,1,0:T(8,128)(2,1)} %param.14) | data formatting | bytes 1835008 | tf_op args[4]
  19.8 0.2 convolution_convert_fusion.1
  20.1 6.1 %collective-permute-done.1 = bf16[1,64,3584]{2,1,0:T(8,128)(2,1)S(1)} collective-permute-done((bf16[1,64,3584]{2,1,0:T(8,128)(2,1)}, bf16[1,64,3584]{2,1,0:T(8,128)(2,1)S(1)}, u32[]{:S(2)}, u32[]{:S(2)}) %collective-permute-start.1) | collective-permute-done | bytes 458784 | tf_op jit(solution)/shard_map/ppermute | solution.py:14
  26.6 1.0 broadcast_in_dim.6
  27.6 1.9 %pad_maximum_fusion.own = bf16[384,3584]{1,0:T(8,128)(2,1)S(1)} fusion(bf16[128,3584]{1,0:T(8,128)(2,1)} %bitcast.33, bf16[128,3584]{1,0:T(8,128)(2,1)} %bitcast.32, bf16[128,3584]{1,0:T(8,128)(2,1)} %bitcast.35), kind=kLoop, calls=%fused_computation.2 | loop fusion | flops 8257536 | bytes 5505024 | tf_op jit(solution)/shard_map/concatenate | solution.py:187
  29.5 1.9 %collective-permute-start.2 = (bf16[384,3584]{1,0:T(8,128)(2,1)S(1)}, bf16[384,3584]{1,0:T(8,128)(2,1)}, u32[]{:S(2)}, u32[]{:S(2)}) collective-permute-start(bf16[384,3584]{1,0:T(8,128)(2,1)S(1)} %pad_maximum_fusion.own), channel_id=1, source_target_pairs={{0,1},{1,0},{2,3},{3,2},{4,5},{5,4},{6,7},{7,6},{8,9},{9,8},{10,11... | collective-permute-start | bytes 8257544 | tf_op jit(solution)/shard_map/ppermute | solution.py:19
  31.5 15.1 %all-to-all-start = ((bf16[24,4,3584]{2,1,0:T(4,128)(2,1)}), bf16[24,4,3584]{2,1,0:T(4,128)(2,1)S(1)}, u32[]{:S(2)}, u32[]{:S(2)}) async-start(bf16[24,4,3584]{2,1,0:T(4,128)(2,1)} %bitcast.34), calls=%async_computation | async-start | bytes 1376256 | tf_op jit(solution)/shard_map/all_to_all | solution.py:185
  46.7 2.1 %collective-permute-start.3 = (bf16[24,2,2,128]{3,1,0,2:T(2,128)(2,1)S(1)}, bf16[24,2,2,128]{3,1,0,2:T(2,128)(2,1)S(1)}, u32[]{:S(2)}, u32[]{:S(2)}) collective-permute-start(bf16[24,2,2,128]{3,1,0,2:T(2,128)(2,1)S(1)} %bitcast.38), channel_id=1, source_target_pairs={{0,1},{1,0},{2,3},{3,2},{4,5},{5,4},{6,7},{7,6},{8,9},{9,8},{10,11... | collective-permute-start | bytes 73736 | tf_op jit(solution)/shard_map/ppermute | solution.py:19
  48.9 0.9 collective-permute-done.3
  49.8 0.7 pad_convert_fusion
  50.5 28.1 %all-to-all-done.rows = bf16[24,4,3584]{2,1,0:T(4,128)(2,1)S(1)} async-done(((bf16[24,4,3584]{2,1,0:T(4,128)(2,1)}), bf16[24,4,3584]{2,1,0:T(4,128)(2,1)S(1)}, u32[]{:S(2)}, u32[]{:S(2)}) %all-to-all-start) | async-done | bytes 688160 | tf_op jit(solution)/shard_map/all_to_all | solution.py:185
  78.6 0.9 copy-done.5
  79.5 5.1 %expert.1 = bf16[24,4,3584]{2,1,0:T(4,128)(2,1)S(1)} custom-call(bf16[24,4,3584]{2,1,0:T(4,128)(2,1)S(1)} %all-to-all-done.rows, bf16[384,3584]{1,0:T(8,128)(2,1)S(1)} %pad_maximum_fusion.own, bf16[384,3584]{1,0:T(8,128)(2,1)} %collective-permute-done.2.other, f32[2,96,128]{2,1,0:T(8,128)S(1)} %bitcast.30, f32[2,96,128]{2,1,0:T(8,128)S(1)} %bitcast.31), custom_call_target="tpu_custom_call" | custom-call | flops 1056964608 | bytes 5505024 | tf_op jit(solution)/shard_map/expert/pallas_call | solution.py:128
  84.6 0.8 copy-done
  85.5 6.8 %all-to-all-start.1 = ((bf16[24,4,3584]{2,1,0:T(4,128)(2,1)}), bf16[24,4,3584]{2,1,0:T(4,128)(2,1)S(1)}, u32[]{:S(2)}, u32[]{:S(2)}) async-start(bf16[24,4,3584]{2,1,0:T(4,128)(2,1)} %copy-done), calls=%async_computation.1 | async-start | bytes 1376256 | tf_op jit(solution)/shard_map/all_to_all | solution.py:198
  92.6 31.4 %all-to-all-done.1.back = bf16[24,4,3584]{2,1,0:T(4,128)(2,1)S(1)} async-done(((bf16[24,4,3584]{2,1,0:T(4,128)(2,1)}), bf16[24,4,3584]{2,1,0:T(4,128)(2,1)S(1)}, u32[]{:S(2)}, u32[]{:S(2)}) %all-to-all-start.1) | async-done | bytes 688160 | tf_op jit(solution)/shard_map/all_to_all | solution.py:198
  124.0 1.0 copy-done.2
  125.0 1.0 copy-done.4
  126.1 2.4 %settle.1 = (bf16[64,3584]{1,0:T(8,128)(2,1)}, bf16[64,3584]{1,0:T(8,128)(2,1)}) custom-call(s32[6]{0:T(128)S(1)} %reshape.37.fwd_slots, f32[6]{0:T(128)S(1)} %reshape.38.fwd_gates, s32[6]{0:T(128)S(1)} %reshape.39.bwd_slots, f32[6]{0:T(128)S(1)} %reshape.40.bwd_gates, bf16[24,4,3584]{2,1,0:T(4,128)(2,1)S(1)} %all-to-all-done.1.back, ...), custom_call_target="tpu_custom_call" | custom-call | flops 688128 | bytes 2293760 | tf_op jit(solution)/shard_map/settle/pallas_call | solution.py:59
  (30 shorter events, 1.1 us)
Async XLA Ops:
  0.6 19.2 %collective-permute-start = (bf16[1,64,3584]{2,1,0:T(8,128)(2,1)}, bf16[1,64,3584]{2,1,0:T(8,128)(2,1)S(1)}, u32[]{:S(2)}, u32[]{:S(2)}) collective-permute-start(bf16[1,64,3584]{2,1,0:T(8,128)(2,1)} %param.10), channel_id=1, source_target_pairs={{0,48},{48,96},{96,144},{144,192},{192,240},{240,288},{288,336},{3... | collective-permute-start | bytes 1376264 | tf_op jit(solution)/shard_map/ppermute | solution.py:14
  11.7 14.5 %collective-permute-start.1 = (bf16[1,64,3584]{2,1,0:T(8,128)(2,1)}, bf16[1,64,3584]{2,1,0:T(8,128)(2,1)S(1)}, u32[]{:S(2)}, u32[]{:S(2)}) collective-permute-start(bf16[1,64,3584]{2,1,0:T(8,128)(2,1)} %param.12), channel_id=1, source_target_pairs={{0,720},{48,0},{96,48},{144,96},{192,144},{240,192},{288,240},{336... | collective-permute-start | bytes 1376264 | tf_op jit(solution)/shard_map/ppermute | solution.py:14
  19.8 7.8 %copy-start.1 = (bf16[1,64,3584]{2,1,0:T(8,128)(2,1)}, bf16[1,64,3584]{2,1,0:T(8,128)(2,1)S(1)}, u32[]{:S(2)}) copy-start(bf16[1,64,3584]{2,1,0:T(8,128)(2,1)S(1)} %collective-permute-done) | copy-start | bytes 1376260
  26.2 1.4 %copy-start.3 = (bf16[1,64,3584]{2,1,0:T(8,128)(2,1)}, bf16[1,64,3584]{2,1,0:T(8,128)(2,1)S(1)}, u32[]{:S(2)}) copy-start(bf16[1,64,3584]{2,1,0:T(8,128)(2,1)S(1)} %collective-permute-done.1) | copy-start | bytes 1376260
  27.6 19.0 %copy-start.6 = (bf16[1,48,2,2,128]{4,3,2,1,0:T(2,128)(2,1)S(1)}, bf16[1,48,2,2,128]{4,3,2,1,0:T(2,128)(2,1)}, u32[]{:S(2)}) copy-start(bf16[1,48,2,2,128]{4,3,2,1,0:T(2,128)(2,1)} %param.11) | copy-start | bytes 147460
  29.5 49.1 %collective-permute-start.2 = (bf16[384,3584]{1,0:T(8,128)(2,1)S(1)}, bf16[384,3584]{1,0:T(8,128)(2,1)}, u32[]{:S(2)}, u32[]{:S(2)}) collective-permute-start(bf16[384,3584]{1,0:T(8,128)(2,1)S(1)} %pad_maximum_fusion.own), channel_id=1, source_target_pairs={{0,1},{1,0},{2,3},{3,2},{4,5},{5,4},{6,7},{7,6},{8,9},{9,8},{10,11... | collective-permute-start | bytes 8257544 | tf_op jit(solution)/shard_map/ppermute | solution.py:19
  31.5 47.1 %all-to-all-start = ((bf16[24,4,3584]{2,1,0:T(4,128)(2,1)}), bf16[24,4,3584]{2,1,0:T(4,128)(2,1)S(1)}, u32[]{:S(2)}, u32[]{:S(2)}) async-start(bf16[24,4,3584]{2,1,0:T(4,128)(2,1)} %bitcast.34), calls=%async_computation | async-start | bytes 1376256 | tf_op jit(solution)/shard_map/all_to_all | solution.py:185
  46.7 3.1 %collective-permute-start.3 = (bf16[24,2,2,128]{3,1,0,2:T(2,128)(2,1)S(1)}, bf16[24,2,2,128]{3,1,0,2:T(2,128)(2,1)S(1)}, u32[]{:S(2)}, u32[]{:S(2)}) collective-permute-start(bf16[24,2,2,128]{3,1,0,2:T(2,128)(2,1)S(1)} %bitcast.38), channel_id=1, source_target_pairs={{0,1},{1,0},{2,3},{3,2},{4,5},{5,4},{6,7},{7,6},{8,9},{9,8},{10,11... | collective-permute-start | bytes 73736 | tf_op jit(solution)/shard_map/ppermute | solution.py:19
  78.6 0.9 copy-start.5
  79.5 12.8 %copy-start.7 = (f32[1,1,3,2]{2,3,1,0:T(2,128)S(1)}, f32[1,1,3,2]{2,3,1,0:T(2,128)}, u32[]{:S(2)}) copy-start(f32[1,1,3,2]{2,3,1,0:T(2,128)} %param.17) | copy-start | bytes 76
  79.5 13.0 %copy-start.8 = (f32[1,1,3,2]{2,3,1,0:T(2,128)S(1)}, f32[1,1,3,2]{2,3,1,0:T(2,128)}, u32[]{:S(2)}) copy-start(f32[1,1,3,2]{2,3,1,0:T(2,128)} %param.19) | copy-start | bytes 76
  84.6 0.9 copy-start
  85.5 38.5 %all-to-all-start.1 = ((bf16[24,4,3584]{2,1,0:T(4,128)(2,1)}), bf16[24,4,3584]{2,1,0:T(4,128)(2,1)S(1)}, u32[]{:S(2)}, u32[]{:S(2)}) async-start(bf16[24,4,3584]{2,1,0:T(4,128)(2,1)} %copy-done), calls=%async_computation.1 | async-start | bytes 1376256 | tf_op jit(solution)/shard_map/all_to_all | solution.py:198
  124.0 1.0 copy-start.2
  125.0 1.0 copy-start.4

commit v6 on v5

--- a/solution.py
+++ b/solution.py
@@ -63,13 +63,13 @@
         in_specs=[smem] * 4 + [pl.BlockSpec((chips, both, step), lambda i: (0, 0, i)), rows, rows],
         out_specs=[rows, rows],
         scratch_shapes=[pltpu.VMEM((tokens + 8, step), jnp.float32)],
-        compiler_params=pltpu.CompilerParams(vmem_limit_bytes=16 * 1024 * 1024),
+        compiler_params=pltpu.CompilerParams(vmem_limit_bytes=16777216),
         cost_estimate=pl.CostEstimate(flops=2 * chips * both * width, bytes_accessed=2560 * width // 4, transcendentals=0),
         name="settle",
     )(fwd_slots, fwd_gates, bwd_slots, bwd_gates, back, inputs, incoming)
 
 
-def expert_kernel(rows, own, other, own_saved, other_saved, out, rows_in, lhs, weights, rows_sem, sems):
+def expert_kernel(rows, own, other_down, other_gate, other_up, own_saved, other_saved, out, rows_in, lhs, weights, saved_in, out_ready, rows_sem, sems, saved_sems, out_sems):
     chips, both, width = rows.shape
     count, piece = own_saved.shape[1:]
     parts = sems.shape[1]
@@ -79,32 +79,38 @@
     rows_copy.start()
     copies = []
     for part in range(parts):
-        for which, source in enumerate((own, other)):
-            copy = pltpu.make_async_copy(
-                source.at[:, columns[part]], weights.at[which, :, columns[part]], sems.at[which, part]
-            )
+        for first, source in ((0, own), (3, other_down), (4, other_gate), (5, other_up)):
+            target = weights.at[pl.ds(first * piece, source.shape[0]), columns[part]]
+            copy = pltpu.make_async_copy(source.at[:, columns[part]], target, sems.at[first, part])
             copy.start()
             copies.append(copy)
+    saved_copies = []
+    for which, source in enumerate((own_saved, other_saved)):
+        copy = pltpu.make_async_copy(source, saved_in.at[which], saved_sems.at[which])
+        copy.start()
+        saved_copies.append(copy)
     rows_copy.wait()
     for chip in range(chips):
         lhs[pl.ds(chip * both, both)] = rows_in[chip].astype(jnp.float32)
-    pre = [jnp.zeros((count, 3 * piece), jnp.float32) for _ in range(2)]
+    pre = jnp.zeros((count, 6 * piece), jnp.float32)
     for part in range(parts):
         left = lhs[:, columns[part]].astype(jnp.bfloat16)
-        for which in range(2):
-            copies[2 * part + which].wait()
-            pre[which] = pre[which] + lax.dot_general(
-                left,
-                weights[which, :, columns[part]],
-                (((1,), (1,)), ((), ())),
-                preferred_element_type=jnp.float32,
-            )
+        for copy in copies[4 * part : 4 * part + 4]:
+            copy.wait()
+        pre = pre + lax.dot_general(
+            left,
+            weights[:, columns[part]],
+            (((1,), (1,)), ((), ())),
+            preferred_element_type=jnp.float32,
+        )
     is_fwd = lax.rem(lax.broadcasted_iota(jnp.int32, (count, piece), 0), both) < both // 2
     acts = []
-    for which, saved in enumerate((own_saved, other_saved)):
-        dh = pre[which][:, :piece]
-        pre_gate = pre[which][:, piece : 2 * piece]
-        pre_up = pre[which][:, 2 * piece :]
+    for which in range(2):
+        saved_copies[which].wait()
+        saved = saved_in[which]
+        dh, pre_gate, pre_up = (
+            pre[:, (3 * which + i) * piece : (3 * which + i + 1) * piece] for i in range(3)
+        )
         hidden = jnp.where(is_fwd, jax.nn.silu(pre_gate) * pre_up, 0.0)
         pre_a = saved[0]
         pre_v = saved[1]
@@ -112,37 +118,49 @@
         slope = sig * (1.0 + pre_a * (1.0 - sig))
         d_gate = dh * pre_v * slope
         d_up = dh * (pre_a * sig)
-        acts.append(jnp.concatenate([hidden, d_gate, d_up], axis=1).astype(jnp.bfloat16))
+        acts += [hidden, d_gate, d_up]
+    acts = jnp.concatenate(acts, axis=1).astype(jnp.bfloat16)
+    out_copies = []
     for part in range(parts):
-        total = jnp.dot(acts[0], weights[0, :, columns[part]], preferred_element_type=jnp.float32)
-        total = total + jnp.dot(acts[1], weights[1, :, columns[part]], preferred_element_type=jnp.float32)
+        total = jnp.dot(acts, weights[:, columns[part]], preferred_element_type=jnp.float32)
         for chip in range(chips):
-            out[chip, :, columns[part]] = total[chip * both : (chip + 1) * both].astype(out.dtype)
-
-
-def expert(rows, own, other, own_saved, other_saved):
+            out_ready[chip, :, columns[part]] = total[chip * both : (chip + 1) * both].astype(out.dtype)
+        copy = pltpu.make_async_copy(
+            out_ready.at[:, :, columns[part]], out.at[:, :, columns[part]], out_sems.at[part]
+        )
+        copy.start()
+        out_copies.append(copy)
+    for copy in out_copies:
+        copy.wait()
+
+
+def expert(rows, own, others, own_saved, other_saved):
     chips, both, width = rows.shape
     parts = 4
-    vmem = pl.BlockSpec(memory_space=pltpu.VMEM)
     anywhere = pl.BlockSpec(memory_space=pl.ANY)
+    hbm = pl.BlockSpec(memory_space=pltpu.HBM)
     return pl.pallas_call(
         expert_kernel,
         out_shape=jax.ShapeDtypeStruct(rows.shape, jnp.bfloat16),
-        in_specs=[anywhere] * 3 + [vmem] * 2,
-        out_specs=vmem,
+        in_specs=[anywhere] + [hbm] * 4 + [anywhere] * 2,
+        out_specs=hbm,
         scratch_shapes=[
             pltpu.VMEM(rows.shape, jnp.bfloat16),
             pltpu.VMEM((chips * both, width), jnp.float32),
-            pltpu.VMEM((2, *own.shape), jnp.bfloat16),
+            pltpu.VMEM((2 * own.shape[0], width), jnp.bfloat16),
+            pltpu.VMEM((2, *own_saved.shape), jnp.float32),
+            pltpu.VMEM(rows.shape, jnp.bfloat16),
             pltpu.SemaphoreType.DMA,
-            pltpu.SemaphoreType.DMA((2, parts)),
+            pltpu.SemaphoreType.DMA((6, parts)),
+            pltpu.SemaphoreType.DMA((2,)),
+            pltpu.SemaphoreType.DMA((parts,)),
         ],
-        compiler_params=pltpu.CompilerParams(vmem_limit_bytes=24 * 1024 * 1024),
+        compiler_params=pltpu.CompilerParams(vmem_limit_bytes=62914560),
         cost_estimate=pl.CostEstimate(
             flops=8 * chips * both * own.size, bytes_accessed=4 * own.size, transcendentals=0
         ),
         name="expert",
-    )(rows, own, other, own_saved, other_saved)
+    )(rows, own, *others, own_saved, other_saved)
 
 
 def local(
@@ -185,7 +203,7 @@
     rows = lax.all_to_all(rows, "expert", 0, 0, axis_index_groups=same_core, tiled=True)
 
     own = jnp.concatenate([w_down, w_gate.T, w_up.T], axis=0)
-    other = swapped(own, "expert")
+    pieces = [swapped(piece, "expert") for piece in jnp.split(own, 3, axis=0)]
     saved = saved.reshape(chips, CORES, cap, 2, hidden_width)
     own_saved = lax.dynamic_index_in_dim(saved, core, 1, keepdims=False)
     other_saved = swapped(lax.dynamic_index_in_dim(saved, 1 - core, 1, keepdims=False), "expert")
@@ -194,7 +212,7 @@
         saved = jnp.concatenate([jnp.zeros_like(saved), saved], axis=1)
         return saved.transpose(2, 0, 1, 3).reshape(2, -1, hidden_width).astype(jnp.float32)
 
-    part = expert(rows, own, other, in_row_order(own_saved), in_row_order(other_saved))
+    part = expert(rows, own, pieces, in_row_order(own_saved), in_row_order(other_saved))
     part = lax.all_to_all(part, "expert", 0, 0, axis_index_groups=same_core, tiled=True)
     fwd_out, grad_out = settle(
         part, fwd_index, fwd_gates.reshape(-1), inputs, bwd_index, bwd_gates.reshape(-1), incoming

time: 129 us -> 121 us (0.938)
  waiting for transfers between devices: 66.5 us -> 55.1 us
  local copies, waits for them, and re-layouts: 11.5 us -> 7.07 us
  starting transfers between devices: 38.9 us -> 42.7 us
  Pallas kernels: 7.54 us -> 10.2 us
  other arithmetic: 2.71 us -> 4.33 us
    all_to_all x1, waiting for transfers between devices: 28.1 us -> 17.9 us  [local(): lax.all_to_all(rows, 'expert', 0, 0, axis_index_groups=same_core, tiled=T...]
    ppermute x2 -> x4, starting transfers between devices: 4.05 us -> 8.66 us  [swapped(): return lax.ppermute(shard, axis, [(i, i ^ 1) for i in range(length)])]
    unnamed x24 -> x14, local copies, waits for them, and re-layouts: 9.98 us -> 5.5 us
    pallas_call x1, Pallas kernels: 5.13 us -> 7.78 us  [expert(): pl.pallas_call(expert_kernel, out_shape=jax.ShapeDtypeStruct(rows.shape,...]
    all_to_all x1, waiting for transfers between devices: 31.4 us -> 29.6 us  [local(): lax.all_to_all(part, 'expert', 0, 0, axis_index_groups=same_core, tiled=T...]
    ppermute x2, waiting for transfers between devices: 6.1 us -> 7.62 us  [shifted(): lax.ppermute(shard, axis, [(i, (i + by) % length) for i in range(length)])]
  transfers between devices with their start and end apart: 6 -> 8, of which waited for: 4 -> 3; matrix products, arithmetic and copies ran while one was open for 6% -> 8% of each run, Pallas kernels for 0% -> 0%
where the time goes in v6:
time: 121 us
  waiting for transfers between devices  55.1 us (46%)
  starting transfers between devices  42.7 us (35%)
  Pallas kernels  10.2 us (8%)
  local copies, waits for them, and re-layouts  7.07 us (6%)
  other arithmetic  4.33 us (4%)
    all_to_all x1, waiting for transfers between devices, local(): lax.all_to_all(part, 'expert', 0, 0, axis_index_groups=same_core, tiled=T...  29.6 us
    all_to_all x1, waiting for transfers between devices, local(): lax.all_to_all(rows, 'expert', 0, 0, axis_index_groups=same_core, tiled=T...  17.9 us
    all_to_all x1, starting transfers between devices, local(): lax.all_to_all(rows, 'expert', 0, 0, axis_index_groups=same_core, tiled=T...  15.1 us
    ppermute x2, starting transfers between devices, shifted(): lax.ppermute(shard, axis, [(i, (i + by) % length) for i in range(length)])  13 us
    ppermute x4, starting transfers between devices, swapped(): return lax.ppermute(shard, axis, [(i, i ^ 1) for i in range(length)])  8.66 us
    pallas_call x1, Pallas kernels, expert(): pl.pallas_call(expert_kernel, out_shape=jax.ShapeDtypeStruct(rows.shape,...  7.78 us
    ppermute x2, waiting for transfers between devices, shifted(): lax.ppermute(shard, axis, [(i, (i + by) % length) for i in range(length)])  7.62 us
    all_to_all x1, starting transfers between devices, local(): lax.all_to_all(part, 'expert', 0, 0, axis_index_groups=same_core, tiled=T...  5.9 us
  transfers between devices with their start and end apart: 8, of which 3 were waited for; matrix products, arithmetic and copies ran while one was open for 8% of the time, Pallas kernels for 0%

profile of v6, /device:TPU:30, one launch (start us, length us, event | category | flops | bytes accessed | tf_op | source)
XLA Modules:
  0.0 120.7 jit_solution(14639196201840283128)
XLA Ops:
  0.6 11.1 %collective-permute-start = (bf16[1,64,3584]{2,1,0:T(8,128)(2,1)}, bf16[1,64,3584]{2,1,0:T(8,128)(2,1)S(1)}, u32[]{:S(2)}, u32[]{:S(2)}) collective-permute-start(bf16[1,64,3584]{2,1,0:T(8,128)(2,1)} %param.10), channel_id=1, source_target_pairs={{0,48},{48,96},{96,144},{144,192},{192,240},{240,288},{288,336},{3... | collective-permute-start | bytes 1376264 | tf_op jit(solution)/shard_map/ppermute | solution.py:14
  11.7 1.9 %collective-permute-start.1 = (bf16[1,64,3584]{2,1,0:T(8,128)(2,1)}, bf16[1,64,3584]{2,1,0:T(8,128)(2,1)S(1)}, u32[]{:S(2)}, u32[]{:S(2)}) collective-permute-start(bf16[1,64,3584]{2,1,0:T(8,128)(2,1)} %param.12), channel_id=1, source_target_pairs={{0,720},{48,0},{96,48},{144,96},{192,144},{240,192},{288,240},{336... | collective-permute-start | bytes 1376264 | tf_op jit(solution)/shard_map/ppermute | solution.py:14
  13.6 0.8 copy.20
  14.5 0.8 copy.22
  15.3 1.5 %copy.24 = bf16[1,3584,128]{1,2,0:T(8,128)(2,1)S(1)} copy(bf16[1,3584,128]{2,1,0:T(8,128)(2,1)} %param.13) | data formatting | bytes 1835008 | tf_op args[3]
  16.8 1.5 %copy.25 = bf16[1,3584,128]{1,2,0:T(8,128)(2,1)S(1)} copy(bf16[1,3584,128]{2,1,0:T(8,128)(2,1)} %param.14) | data formatting | bytes 1835008 | tf_op args[4]
  18.3 0.2 convolution_convert_fusion.1
  18.6 7.6 %collective-permute-done.1 = bf16[1,64,3584]{2,1,0:T(8,128)(2,1)S(1)} collective-permute-done((bf16[1,64,3584]{2,1,0:T(8,128)(2,1)}, bf16[1,64,3584]{2,1,0:T(8,128)(2,1)S(1)}, u32[]{:S(2)}, u32[]{:S(2)}) %collective-permute-start.1) | collective-permute-done | bytes 458784 | tf_op jit(solution)/shard_map/ppermute | solution.py:14
  26.2 0.2 convolution_convert_fusion
  26.6 1.0 broadcast_in_dim.6
  27.6 15.1 %all-to-all-start = ((bf16[24,4,3584]{2,1,0:T(4,128)(2,1)}), bf16[24,4,3584]{2,1,0:T(4,128)(2,1)S(1)}, u32[]{:S(2)}, u32[]{:S(2)}) async-start(bf16[24,4,3584]{2,1,0:T(4,128)(2,1)} %bitcast.34), calls=%async_computation | async-start | bytes 1376256 | tf_op jit(solution)/shard_map/all_to_all | solution.py:203
  42.7 1.9 %collective-permute-start.2 = (bf16[128,3584]{1,0:T(8,128)(2,1)}, bf16[128,3584]{1,0:T(8,128)(2,1)}, u32[]{:S(2)}, u32[]{:S(2)}) collective-permute-start(bf16[128,3584]{1,0:T(8,128)(2,1)} %bitcast.35), channel_id=1, source_target_pairs={{0,1},{1,0},{2,3},{3,2},{4,5},{5,4},{6,7},{7,6},{8,9},{9,8},{10,11... | collective-permute-start | bytes 2752520 | tf_op jit(solution)/shard_map/ppermute | solution.py:19
  44.7 2.4 %collective-permute-start.3 = (bf16[128,3584]{1,0:T(8,128)(2,1)S(1)}, bf16[128,3584]{1,0:T(8,128)(2,1)}, u32[]{:S(2)}, u32[]{:S(2)}) collective-permute-start(bf16[128,3584]{1,0:T(8,128)(2,1)S(1)} %bitcast.32), channel_id=1, source_target_pairs={{0,1},{1,0},{2,3},{3,2},{4,5},{5,4},{6,7},{7,6},{8,9},{9,8},{10,11... | collective-permute-start | bytes 2752520 | tf_op jit(solution)/shard_map/ppermute | solution.py:19
  47.1 1.9 %collective-permute-start.4 = (bf16[128,3584]{1,0:T(8,128)(2,1)S(1)}, bf16[128,3584]{1,0:T(8,128)(2,1)}, u32[]{:S(2)}, u32[]{:S(2)}) collective-permute-start(bf16[128,3584]{1,0:T(8,128)(2,1)S(1)} %bitcast.30), channel_id=1, source_target_pairs={{0,1},{1,0},{2,3},{3,2},{4,5},{5,4},{6,7},{7,6},{8,9},{9,8},{10,11... | collective-permute-start | bytes 2752520 | tf_op jit(solution)/shard_map/ppermute | solution.py:19
  49.1 2.4 %collective-permute-start.5 = (bf16[24,2,2,128]{3,1,0,2:T(2,128)(2,1)S(1)}, bf16[24,2,2,128]{3,1,0,2:T(2,128)(2,1)S(1)}, u32[]{:S(2)}, u32[]{:S(2)}) collective-permute-start(bf16[24,2,2,128]{3,1,0,2:T(2,128)(2,1)S(1)} %bitcast.41), channel_id=1, source_target_pairs={{0,1},{1,0},{2,3},{3,2},{4,5},{5,4},{6,7},{7,6},{8,9},{9,8},{10,11... | collective-permute-start | bytes 73736 | tf_op jit(solution)/shard_map/ppermute | solution.py:19
  51.6 2.9 %pad_maximum_fusion.own = bf16[384,3584]{1,0:T(8,128)(2,1)} fusion(bf16[128,3584]{1,0:T(8,128)(2,1)S(1)} %bitcast.31, bf16[128,3584]{1,0:T(8,128)(2,1)S(1)} %bitcast.33, bf16[128,3584]{1,0:T(8,128)(2,1)} %bitcast.36), kind=kLoop, calls=%fused_computation.2 | loop fusion | flops 8257536 | bytes 5505024 | tf_op jit(solution)/shard_map/concatenate | solution.py:205
  54.5 0.7 pad_convert_fusion.1
  55.1 0.7 pad_convert_fusion
  55.8 17.9 %all-to-all-done.rows = bf16[24,4,3584]{2,1,0:T(4,128)(2,1)S(1)} async-done(((bf16[24,4,3584]{2,1,0:T(4,128)(2,1)}), bf16[24,4,3584]{2,1,0:T(4,128)(2,1)S(1)}, u32[]{:S(2)}, u32[]{:S(2)}) %all-to-all-start) | async-done | bytes 688160 | tf_op jit(solution)/shard_map/all_to_all | solution.py:203
  73.7 0.9 copy-done
  74.6 7.8 %expert.1 = bf16[24,4,3584]{2,1,0:T(4,128)(2,1)} custom-call(bf16[24,4,3584]{2,1,0:T(4,128)(2,1)} %copy-done, bf16[384,3584]{1,0:T(8,128)(2,1)} %pad_maximum_fusion.own, bf16[128,3584]{1,0:T(8,128)(2,1)} %collective-permute-done.2.other_down, bf16[128,3584]{1,0:T(8,128)(2,1)} %collective-permute-done.3.other_gate, ...), custom_call_target="tpu_custom_call" | custom-call | flops 1056964608 | bytes 5505024 | tf_op jit(solution)/shard_map/expert/pallas_call | solution.py:142
  82.4 5.9 %all-to-all-start.1 = ((bf16[24,4,3584]{2,1,0:T(4,128)(2,1)}), bf16[24,4,3584]{2,1,0:T(4,128)(2,1)S(1)}, u32[]{:S(2)}, u32[]{:S(2)}) async-start(bf16[24,4,3584]{2,1,0:T(4,128)(2,1)} %expert.1), calls=%async_computation.1 | async-start | bytes 1376256 | tf_op jit(solution)/shard_map/all_to_all | solution.py:216
  88.7 29.6 %all-to-all-done.1.back = bf16[24,4,3584]{2,1,0:T(4,128)(2,1)S(1)} async-done(((bf16[24,4,3584]{2,1,0:T(4,128)(2,1)}), bf16[24,4,3584]{2,1,0:T(4,128)(2,1)S(1)}, u32[]{:S(2)}, u32[]{:S(2)}) %all-to-all-start.1) | async-done | bytes 688160 | tf_op jit(solution)/shard_map/all_to_all | solution.py:216
  118.3 2.4 %settle.1 = (bf16[64,3584]{1,0:T(8,128)(2,1)}, bf16[64,3584]{1,0:T(8,128)(2,1)}) custom-call(s32[6]{0:T(128)S(1)} %reshape.37.fwd_slots, f32[6]{0:T(128)S(1)} %reshape.38.fwd_gates, s32[6]{0:T(128)S(1)} %reshape.39.bwd_slots, f32[6]{0:T(128)S(1)} %reshape.40.bwd_gates, bf16[24,4,3584]{2,1,0:T(4,128)(2,1)S(1)} %all-to-all-done.1.back, ...), custom_call_target="tpu_custom_call" | custom-call | flops 688128 | bytes 2293760 | tf_op jit(solution)/shard_map/settle/pallas_call | solution.py:59
  (24 shorter events, 0.8 us)
Async XLA Ops:
  0.6 17.6 %collective-permute-start = (bf16[1,64,3584]{2,1,0:T(8,128)(2,1)}, bf16[1,64,3584]{2,1,0:T(8,128)(2,1)S(1)}, u32[]{:S(2)}, u32[]{:S(2)}) collective-permute-start(bf16[1,64,3584]{2,1,0:T(8,128)(2,1)} %param.10), channel_id=1, source_target_pairs={{0,48},{48,96},{96,144},{144,192},{192,240},{240,288},{288,336},{3... | collective-permute-start | bytes 1376264 | tf_op jit(solution)/shard_map/ppermute | solution.py:14
  11.7 14.5 %collective-permute-start.1 = (bf16[1,64,3584]{2,1,0:T(8,128)(2,1)}, bf16[1,64,3584]{2,1,0:T(8,128)(2,1)S(1)}, u32[]{:S(2)}, u32[]{:S(2)}) collective-permute-start(bf16[1,64,3584]{2,1,0:T(8,128)(2,1)} %param.12), channel_id=1, source_target_pairs={{0,720},{48,0},{96,48},{144,96},{192,144},{240,192},{288,240},{336... | collective-permute-start | bytes 1376264 | tf_op jit(solution)/shard_map/ppermute | solution.py:14
  16.8 32.3 %copy-start.1 = (bf16[1,48,2,2,128]{4,3,2,1,0:T(2,128)(2,1)S(1)}, bf16[1,48,2,2,128]{4,3,2,1,0:T(2,128)(2,1)}, u32[]{:S(2)}) copy-start(bf16[1,48,2,2,128]{4,3,2,1,0:T(2,128)(2,1)} %param.11) | copy-start | bytes 147460
  27.6 46.1 %all-to-all-start = ((bf16[24,4,3584]{2,1,0:T(4,128)(2,1)}), bf16[24,4,3584]{2,1,0:T(4,128)(2,1)S(1)}, u32[]{:S(2)}, u32[]{:S(2)}) async-start(bf16[24,4,3584]{2,1,0:T(4,128)(2,1)} %bitcast.34), calls=%async_computation | async-start | bytes 1376256 | tf_op jit(solution)/shard_map/all_to_all | solution.py:203
  42.7 13.1 %collective-permute-start.2 = (bf16[128,3584]{1,0:T(8,128)(2,1)}, bf16[128,3584]{1,0:T(8,128)(2,1)}, u32[]{:S(2)}, u32[]{:S(2)}) collective-permute-start(bf16[128,3584]{1,0:T(8,128)(2,1)} %bitcast.35), channel_id=1, source_target_pairs={{0,1},{1,0},{2,3},{3,2},{4,5},{5,4},{6,7},{7,6},{8,9},{9,8},{10,11... | collective-permute-start | bytes 2752520 | tf_op jit(solution)/shard_map/ppermute | solution.py:19
  44.7 11.1 %collective-permute-start.3 = (bf16[128,3584]{1,0:T(8,128)(2,1)S(1)}, bf16[128,3584]{1,0:T(8,128)(2,1)}, u32[]{:S(2)}, u32[]{:S(2)}) collective-permute-start(bf16[128,3584]{1,0:T(8,128)(2,1)S(1)} %bitcast.32), channel_id=1, source_target_pairs={{0,1},{1,0},{2,3},{3,2},{4,5},{5,4},{6,7},{7,6},{8,9},{9,8},{10,11... | collective-permute-start | bytes 2752520 | tf_op jit(solution)/shard_map/ppermute | solution.py:19
  47.1 8.7 %collective-permute-start.4 = (bf16[128,3584]{1,0:T(8,128)(2,1)S(1)}, bf16[128,3584]{1,0:T(8,128)(2,1)}, u32[]{:S(2)}, u32[]{:S(2)}) collective-permute-start(bf16[128,3584]{1,0:T(8,128)(2,1)S(1)} %bitcast.30), channel_id=1, source_target_pairs={{0,1},{1,0},{2,3},{3,2},{4,5},{5,4},{6,7},{7,6},{8,9},{9,8},{10,11... | collective-permute-start | bytes 2752520 | tf_op jit(solution)/shard_map/ppermute | solution.py:19
  49.1 6.0 %collective-permute-start.5 = (bf16[24,2,2,128]{3,1,0,2:T(2,128)(2,1)S(1)}, bf16[24,2,2,128]{3,1,0,2:T(2,128)(2,1)S(1)}, u32[]{:S(2)}, u32[]{:S(2)}) collective-permute-start(bf16[24,2,2,128]{3,1,0,2:T(2,128)(2,1)S(1)} %bitcast.41), channel_id=1, source_target_pairs={{0,1},{1,0},{2,3},{3,2},{4,5},{5,4},{6,7},{7,6},{8,9},{9,8},{10,11... | collective-permute-start | bytes 73736 | tf_op jit(solution)/shard_map/ppermute | solution.py:19
  73.7 0.9 copy-start
  74.6 13.7 %copy-start.2 = (f32[1,1,3,2]{2,3,1,0:T(2,128)S(1)}, f32[1,1,3,2]{2,3,1,0:T(2,128)}, u32[]{:S(2)}) copy-start(f32[1,1,3,2]{2,3,1,0:T(2,128)} %param.17) | copy-start | bytes 76
  74.6 13.9 %copy-start.3 = (f32[1,1,3,2]{2,3,1,0:T(2,128)S(1)}, f32[1,1,3,2]{2,3,1,0:T(2,128)}, u32[]{:S(2)}) copy-start(f32[1,1,3,2]{2,3,1,0:T(2,128)} %param.19) | copy-start | bytes 76
  82.4 35.9 %all-to-all-start.1 = ((bf16[24,4,3584]{2,1,0:T(4,128)(2,1)}), bf16[24,4,3584]{2,1,0:T(4,128)(2,1)S(1)}, u32[]{:S(2)}, u32[]{:S(2)}) async-start(bf16[24,4,3584]{2,1,0:T(4,128)(2,1)} %expert.1), calls=%async_computation.1 | async-start | bytes 1376256 | tf_op jit(solution)/shard_map/all_to_all | solution.py:216

commit v7 on v6

--- a/solution.py
+++ b/solution.py
@@ -7,6 +7,7 @@
 
 CORES = 2
 GROUPS = 3
+AHEAD = 2
 
 
 def shifted(shard, axis, by):
@@ -81,9 +82,9 @@
     for part in range(parts):
         for first, source in ((0, own), (3, other_down), (4, other_gate), (5, other_up)):
             target = weights.at[pl.ds(first * piece, source.shape[0]), columns[part]]
-            copy = pltpu.make_async_copy(source.at[:, columns[part]], target, sems.at[first, part])
-            copy.start()
-            copies.append(copy)
+            copies.append(pltpu.make_async_copy(source.at[:, columns[part]], target, sems.at[first, part]))
+    for copy in copies[: 4 * AHEAD]:
+        copy.start()
     saved_copies = []
     for which, source in enumerate((own_saved, other_saved)):
         copy = pltpu.make_async_copy(source, saved_in.at[which], saved_sems.at[which])
@@ -92,17 +93,20 @@
     rows_copy.wait()
     for chip in range(chips):
         lhs[pl.ds(chip * both, both)] = rows_in[chip].astype(jnp.float32)
-    pre = jnp.zeros((count, 6 * piece), jnp.float32)
+    pre = jnp.zeros((6 * piece, count), jnp.float32)
     for part in range(parts):
         left = lhs[:, columns[part]].astype(jnp.bfloat16)
         for copy in copies[4 * part : 4 * part + 4]:
             copy.wait()
+        for copy in copies[4 * (part + AHEAD) : 4 * (part + AHEAD) + 4]:
+            copy.start()
         pre = pre + lax.dot_general(
+            weights[:, columns[part]],
             left,
-            weights[:, columns[part]],
             (((1,), (1,)), ((), ())),
             preferred_element_type=jnp.float32,
         )
+    pre = pre.T
     is_fwd = lax.rem(lax.broadcasted_iota(jnp.int32, (count, piece), 0), both) < both // 2
     acts = []
     for which in range(2):

time: 121 us -> 121 us (level)
  no operation moved by 1% of the time
where the time goes in v7:
time: 121 us; the launch traced here: 120 us
  waiting for transfers between devices  55.1 us (46%)
  starting transfers between devices  42.6 us (35%)
  Pallas kernels  9.42 us (8%)
  local copies, waits for them, and re-layouts  7.07 us (6%)
  other arithmetic  4.33 us (4%)
    all_to_all x1, waiting for transfers between devices, local(): lax.all_to_all(part, 'expert', 0, 0, axis_index_groups=same_core, tiled=T...  29.6 us
    all_to_all x1, waiting for transfers between devices, local(): lax.all_to_all(rows, 'expert', 0, 0, axis_index_groups=same_core, tiled=T...  17.9 us
    all_to_all x1, starting transfers between devices, local(): lax.all_to_all(rows, 'expert', 0, 0, axis_index_groups=same_core, tiled=T...  15.1 us
    ppermute x2, starting transfers between devices, shifted(): lax.ppermute(shard, axis, [(i, (i + by) % length) for i in range(length)])  13 us
    ppermute x4, starting transfers between devices, swapped(): return lax.ppermute(shard, axis, [(i, i ^ 1) for i in range(length)])  8.66 us
    ppermute x2, waiting for transfers between devices, shifted(): lax.ppermute(shard, axis, [(i, (i + by) % length) for i in range(length)])  7.62 us
    pallas_call x1, Pallas kernels, expert(): pl.pallas_call(expert_kernel, out_shape=jax.ShapeDtypeStruct(rows.shape,...  7.01 us
    all_to_all x1, starting transfers between devices, local(): lax.all_to_all(part, 'expert', 0, 0, axis_index_groups=same_core, tiled=T...  5.89 us
  transfers between devices with their start and end apart: 8, of which 3 were waited for; matrix products, arithmetic and copies ran while one was open for 8% of the time, Pallas kernels for 0%

profile of v7, /device:TPU:30, one launch (start us, length us, event | category | flops | bytes accessed | tf_op | source)
XLA Modules:
  0.0 119.9 jit_solution(4196437756995578367)
XLA Ops:
  0.6 11.1 %collective-permute-start = (bf16[1,64,3584]{2,1,0:T(8,128)(2,1)}, bf16[1,64,3584]{2,1,0:T(8,128)(2,1)S(1)}, u32[]{:S(2)}, u32[]{:S(2)}) collective-permute-start(bf16[1,64,3584]{2,1,0:T(8,128)(2,1)} %param.10), channel_id=1, source_target_pairs={{0,48},{48,96},{96,144},{144,192},{192,240},{240,288},{288,336},{3... | collective-permute-start | bytes 1376264 | tf_op jit(solution)/shard_map/ppermute | solution.py:15
  11.7 1.9 %collective-permute-start.1 = (bf16[1,64,3584]{2,1,0:T(8,128)(2,1)}, bf16[1,64,3584]{2,1,0:T(8,128)(2,1)S(1)}, u32[]{:S(2)}, u32[]{:S(2)}) collective-permute-start(bf16[1,64,3584]{2,1,0:T(8,128)(2,1)} %param.12), channel_id=1, source_target_pairs={{0,720},{48,0},{96,48},{144,96},{192,144},{240,192},{288,240},{336... | collective-permute-start | bytes 1376264 | tf_op jit(solution)/shard_map/ppermute | solution.py:15
  13.6 0.8 copy.20
  14.5 0.8 copy.22
  15.3 1.5 %copy.24 = bf16[1,3584,128]{1,2,0:T(8,128)(2,1)S(1)} copy(bf16[1,3584,128]{2,1,0:T(8,128)(2,1)} %param.13) | data formatting | bytes 1835008 | tf_op args[3]
  16.8 1.5 %copy.25 = bf16[1,3584,128]{1,2,0:T(8,128)(2,1)S(1)} copy(bf16[1,3584,128]{2,1,0:T(8,128)(2,1)} %param.14) | data formatting | bytes 1835008 | tf_op args[4]
  18.3 0.2 convolution_convert_fusion.1
  18.6 7.6 %collective-permute-done.1 = bf16[1,64,3584]{2,1,0:T(8,128)(2,1)S(1)} collective-permute-done((bf16[1,64,3584]{2,1,0:T(8,128)(2,1)}, bf16[1,64,3584]{2,1,0:T(8,128)(2,1)S(1)}, u32[]{:S(2)}, u32[]{:S(2)}) %collective-permute-start.1) | collective-permute-done | bytes 458784 | tf_op jit(solution)/shard_map/ppermute | solution.py:15
  26.2 0.2 convolution_convert_fusion
  26.6 1.0 broadcast_in_dim.6
  27.6 15.1 %all-to-all-start = ((bf16[24,4,3584]{2,1,0:T(4,128)(2,1)}), bf16[24,4,3584]{2,1,0:T(4,128)(2,1)S(1)}, u32[]{:S(2)}, u32[]{:S(2)}) async-start(bf16[24,4,3584]{2,1,0:T(4,128)(2,1)} %bitcast.34), calls=%async_computation | async-start | bytes 1376256 | tf_op jit(solution)/shard_map/all_to_all | solution.py:207
  42.7 1.9 %collective-permute-start.2 = (bf16[128,3584]{1,0:T(8,128)(2,1)}, bf16[128,3584]{1,0:T(8,128)(2,1)}, u32[]{:S(2)}, u32[]{:S(2)}) collective-permute-start(bf16[128,3584]{1,0:T(8,128)(2,1)} %bitcast.35), channel_id=1, source_target_pairs={{0,1},{1,0},{2,3},{3,2},{4,5},{5,4},{6,7},{7,6},{8,9},{9,8},{10,11... | collective-permute-start | bytes 2752520 | tf_op jit(solution)/shard_map/ppermute | solution.py:20
  44.7 2.4 %collective-permute-start.3 = (bf16[128,3584]{1,0:T(8,128)(2,1)S(1)}, bf16[128,3584]{1,0:T(8,128)(2,1)}, u32[]{:S(2)}, u32[]{:S(2)}) collective-permute-start(bf16[128,3584]{1,0:T(8,128)(2,1)S(1)} %bitcast.32), channel_id=1, source_target_pairs={{0,1},{1,0},{2,3},{3,2},{4,5},{5,4},{6,7},{7,6},{8,9},{9,8},{10,11... | collective-permute-start | bytes 2752520 | tf_op jit(solution)/shard_map/ppermute | solution.py:20
  47.1 1.9 %collective-permute-start.4 = (bf16[128,3584]{1,0:T(8,128)(2,1)S(1)}, bf16[128,3584]{1,0:T(8,128)(2,1)}, u32[]{:S(2)}, u32[]{:S(2)}) collective-permute-start(bf16[128,3584]{1,0:T(8,128)(2,1)S(1)} %bitcast.30), channel_id=1, source_target_pairs={{0,1},{1,0},{2,3},{3,2},{4,5},{5,4},{6,7},{7,6},{8,9},{9,8},{10,11... | collective-permute-start | bytes 2752520 | tf_op jit(solution)/shard_map/ppermute | solution.py:20
  49.1 2.4 %collective-permute-start.5 = (bf16[24,2,2,128]{3,1,0,2:T(2,128)(2,1)S(1)}, bf16[24,2,2,128]{3,1,0,2:T(2,128)(2,1)S(1)}, u32[]{:S(2)}, u32[]{:S(2)}) collective-permute-start(bf16[24,2,2,128]{3,1,0,2:T(2,128)(2,1)S(1)} %bitcast.41), channel_id=1, source_target_pairs={{0,1},{1,0},{2,3},{3,2},{4,5},{5,4},{6,7},{7,6},{8,9},{9,8},{10,11... | collective-permute-start | bytes 73736 | tf_op jit(solution)/shard_map/ppermute | solution.py:20
  51.6 2.9 %pad_maximum_fusion.own = bf16[384,3584]{1,0:T(8,128)(2,1)} fusion(bf16[128,3584]{1,0:T(8,128)(2,1)S(1)} %bitcast.31, bf16[128,3584]{1,0:T(8,128)(2,1)S(1)} %bitcast.33, bf16[128,3584]{1,0:T(8,128)(2,1)} %bitcast.36), kind=kLoop, calls=%fused_computation.2 | loop fusion | flops 8257536 | bytes 5505024 | tf_op jit(solution)/shard_map/concatenate | solution.py:209
  54.5 0.7 pad_convert_fusion.1
  55.1 0.7 pad_convert_fusion
  55.8 17.9 %all-to-all-done.rows = bf16[24,4,3584]{2,1,0:T(4,128)(2,1)S(1)} async-done(((bf16[24,4,3584]{2,1,0:T(4,128)(2,1)}), bf16[24,4,3584]{2,1,0:T(4,128)(2,1)S(1)}, u32[]{:S(2)}, u32[]{:S(2)}) %all-to-all-start) | async-done | bytes 688160 | tf_op jit(solution)/shard_map/all_to_all | solution.py:207
  73.7 0.9 copy-done
  74.6 7.0 %expert.1 = bf16[24,4,3584]{2,1,0:T(4,128)(2,1)} custom-call(bf16[24,4,3584]{2,1,0:T(4,128)(2,1)} %copy-done, bf16[384,3584]{1,0:T(8,128)(2,1)} %pad_maximum_fusion.own, bf16[128,3584]{1,0:T(8,128)(2,1)} %collective-permute-done.2.other_down, bf16[128,3584]{1,0:T(8,128)(2,1)} %collective-permute-done.3.other_gate, ...), custom_call_target="tpu_custom_call" | custom-call | flops 1056964608 | bytes 5505024 | tf_op jit(solution)/shard_map/expert/pallas_call | solution.py:146
  81.6 5.9 %all-to-all-start.1 = ((bf16[24,4,3584]{2,1,0:T(4,128)(2,1)}), bf16[24,4,3584]{2,1,0:T(4,128)(2,1)S(1)}, u32[]{:S(2)}, u32[]{:S(2)}) async-start(bf16[24,4,3584]{2,1,0:T(4,128)(2,1)} %expert.1), calls=%async_computation.1 | async-start | bytes 1376256 | tf_op jit(solution)/shard_map/all_to_all | solution.py:220
  87.9 29.6 %all-to-all-done.1.back = bf16[24,4,3584]{2,1,0:T(4,128)(2,1)S(1)} async-done(((bf16[24,4,3584]{2,1,0:T(4,128)(2,1)}), bf16[24,4,3584]{2,1,0:T(4,128)(2,1)S(1)}, u32[]{:S(2)}, u32[]{:S(2)}) %all-to-all-start.1) | async-done | bytes 688160 | tf_op jit(solution)/shard_map/all_to_all | solution.py:220
  117.5 2.4 %settle.1 = (bf16[64,3584]{1,0:T(8,128)(2,1)}, bf16[64,3584]{1,0:T(8,128)(2,1)}) custom-call(s32[6]{0:T(128)S(1)} %reshape.37.fwd_slots, f32[6]{0:T(128)S(1)} %reshape.38.fwd_gates, s32[6]{0:T(128)S(1)} %reshape.39.bwd_slots, f32[6]{0:T(128)S(1)} %reshape.40.bwd_gates, bf16[24,4,3584]{2,1,0:T(4,128)(2,1)S(1)} %all-to-all-done.1.back, ...), custom_call_target="tpu_custom_call" | custom-call | flops 688128 | bytes 2293760 | tf_op jit(solution)/shard_map/settle/pallas_call | solution.py:60
  (24 shorter events, 0.8 us)
Async XLA Ops:
  0.6 17.6 %collective-permute-start = (bf16[1,64,3584]{2,1,0:T(8,128)(2,1)}, bf16[1,64,3584]{2,1,0:T(8,128)(2,1)S(1)}, u32[]{:S(2)}, u32[]{:S(2)}) collective-permute-start(bf16[1,64,3584]{2,1,0:T(8,128)(2,1)} %param.10), channel_id=1, source_target_pairs={{0,48},{48,96},{96,144},{144,192},{192,240},{240,288},{288,336},{3... | collective-permute-start | bytes 1376264 | tf_op jit(solution)/shard_map/ppermute | solution.py:15
  11.7 14.5 %collective-permute-start.1 = (bf16[1,64,3584]{2,1,0:T(8,128)(2,1)}, bf16[1,64,3584]{2,1,0:T(8,128)(2,1)S(1)}, u32[]{:S(2)}, u32[]{:S(2)}) collective-permute-start(bf16[1,64,3584]{2,1,0:T(8,128)(2,1)} %param.12), channel_id=1, source_target_pairs={{0,720},{48,0},{96,48},{144,96},{192,144},{240,192},{288,240},{336... | collective-permute-start | bytes 1376264 | tf_op jit(solution)/shard_map/ppermute | solution.py:15
  16.8 32.3 %copy-start.1 = (bf16[1,48,2,2,128]{4,3,2,1,0:T(2,128)(2,1)S(1)}, bf16[1,48,2,2,128]{4,3,2,1,0:T(2,128)(2,1)}, u32[]{:S(2)}) copy-start(bf16[1,48,2,2,128]{4,3,2,1,0:T(2,128)(2,1)} %param.11) | copy-start | bytes 147460
  27.6 46.1 %all-to-all-start = ((bf16[24,4,3584]{2,1,0:T(4,128)(2,1)}), bf16[24,4,3584]{2,1,0:T(4,128)(2,1)S(1)}, u32[]{:S(2)}, u32[]{:S(2)}) async-start(bf16[24,4,3584]{2,1,0:T(4,128)(2,1)} %bitcast.34), calls=%async_computation | async-start | bytes 1376256 | tf_op jit(solution)/shard_map/all_to_all | solution.py:207
  42.7 13.1 %collective-permute-start.2 = (bf16[128,3584]{1,0:T(8,128)(2,1)}, bf16[128,3584]{1,0:T(8,128)(2,1)}, u32[]{:S(2)}, u32[]{:S(2)}) collective-permute-start(bf16[128,3584]{1,0:T(8,128)(2,1)} %bitcast.35), channel_id=1, source_target_pairs={{0,1},{1,0},{2,3},{3,2},{4,5},{5,4},{6,7},{7,6},{8,9},{9,8},{10,11... | collective-permute-start | bytes 2752520 | tf_op jit(solution)/shard_map/ppermute | solution.py:20
  44.7 11.1 %collective-permute-start.3 = (bf16[128,3584]{1,0:T(8,128)(2,1)S(1)}, bf16[128,3584]{1,0:T(8,128)(2,1)}, u32[]{:S(2)}, u32[]{:S(2)}) collective-permute-start(bf16[128,3584]{1,0:T(8,128)(2,1)S(1)} %bitcast.32), channel_id=1, source_target_pairs={{0,1},{1,0},{2,3},{3,2},{4,5},{5,4},{6,7},{7,6},{8,9},{9,8},{10,11... | collective-permute-start | bytes 2752520 | tf_op jit(solution)/shard_map/ppermute | solution.py:20
  47.1 8.7 %collective-permute-start.4 = (bf16[128,3584]{1,0:T(8,128)(2,1)S(1)}, bf16[128,3584]{1,0:T(8,128)(2,1)}, u32[]{:S(2)}, u32[]{:S(2)}) collective-permute-start(bf16[128,3584]{1,0:T(8,128)(2,1)S(1)} %bitcast.30), channel_id=1, source_target_pairs={{0,1},{1,0},{2,3},{3,2},{4,5},{5,4},{6,7},{7,6},{8,9},{9,8},{10,11... | collective-permute-start | bytes 2752520 | tf_op jit(solution)/shard_map/ppermute | solution.py:20
  49.1 6.0 %collective-permute-start.5 = (bf16[24,2,2,128]{3,1,0,2:T(2,128)(2,1)S(1)}, bf16[24,2,2,128]{3,1,0,2:T(2,128)(2,1)S(1)}, u32[]{:S(2)}, u32[]{:S(2)}) collective-permute-start(bf16[24,2,2,128]{3,1,0,2:T(2,128)(2,1)S(1)} %bitcast.41), channel_id=1, source_target_pairs={{0,1},{1,0},{2,3},{3,2},{4,5},{5,4},{6,7},{7,6},{8,9},{9,8},{10,11... | collective-permute-start | bytes 73736 | tf_op jit(solution)/shard_map/ppermute | solution.py:20
  73.7 0.9 copy-start
  74.6 12.9 %copy-start.2 = (f32[1,1,3,2]{2,3,1,0:T(2,128)S(1)}, f32[1,1,3,2]{2,3,1,0:T(2,128)}, u32[]{:S(2)}) copy-start(f32[1,1,3,2]{2,3,1,0:T(2,128)} %param.17) | copy-start | bytes 76
  74.6 13.1 %copy-start.3 = (f32[1,1,3,2]{2,3,1,0:T(2,128)S(1)}, f32[1,1,3,2]{2,3,1,0:T(2,128)}, u32[]{:S(2)}) copy-start(f32[1,1,3,2]{2,3,1,0:T(2,128)} %param.19) | copy-start | bytes 76
  81.6 35.9 %all-to-all-start.1 = ((bf16[24,4,3584]{2,1,0:T(4,128)(2,1)}), bf16[24,4,3584]{2,1,0:T(4,128)(2,1)S(1)}, u32[]{:S(2)}, u32[]{:S(2)}) async-start(bf16[24,4,3584]{2,1,0:T(4,128)(2,1)} %expert.1), calls=%async_computation.1 | async-start | bytes 1376256 | tf_op jit(solution)/shard_map/all_to_all | solution.py:220

commit v8 on v7

--- a/solution.py
+++ b/solution.py
@@ -54,7 +54,7 @@
 def settle(back, fwd_slots, fwd_gates, inputs, bwd_slots, bwd_gates, incoming):
     chips, both, width = back.shape
     tokens = inputs.shape[0]
-    step = width // 4
+    step = width
     smem = pl.BlockSpec(memory_space=pltpu.SMEM)
     rows = pl.BlockSpec((tokens, step), lambda i: (0, i))
     return pl.pallas_call(

time: 121 us -> 120 us (level)
  no operation moved by 1% of the time
where the time goes in v8:
time: 120 us; the launch traced here: 119 us
  waiting for transfers between devices  55.1 us (46%)
  starting transfers between devices  42.6 us (36%)
  Pallas kernels  8.78 us (7%)
  local copies, waits for them, and re-layouts  7.07 us (6%)
  other arithmetic  4.33 us (4%)
    all_to_all x1, waiting for transfers between devices, local(): lax.all_to_all(part, 'expert', 0, 0, axis_index_groups=same_core, tiled=T...  29.6 us
    all_to_all x1, waiting for transfers between devices, local(): lax.all_to_all(rows, 'expert', 0, 0, axis_index_groups=same_core, tiled=T...  17.9 us
    all_to_all x1, starting transfers between devices, local(): lax.all_to_all(rows, 'expert', 0, 0, axis_index_groups=same_core, tiled=T...  15.1 us
    ppermute x2, starting transfers between devices, shifted(): lax.ppermute(shard, axis, [(i, (i + by) % length) for i in range(length)])  13 us
    ppermute x4, starting transfers between devices, swapped(): return lax.ppermute(shard, axis, [(i, i ^ 1) for i in range(length)])  8.66 us
    ppermute x2, waiting for transfers between devices, shifted(): lax.ppermute(shard, axis, [(i, (i + by) % length) for i in range(length)])  7.62 us
    pallas_call x1, Pallas kernels, expert(): pl.pallas_call(expert_kernel, out_shape=jax.ShapeDtypeStruct(rows.shape,...  7.01 us
    all_to_all x1, starting transfers between devices, local(): lax.all_to_all(part, 'expert', 0, 0, axis_index_groups=same_core, tiled=T...  5.89 us
  transfers between devices with their start and end apart: 8, of which 3 were waited for; matrix products, arithmetic and copies ran while one was open for 8% of the time, Pallas kernels for 0%

profile of v8, /device:TPU:30, one launch (start us, length us, event | category | flops | bytes accessed | tf_op | source)
XLA Modules:
  0.0 119.3 jit_solution(10752898429148568487)
XLA Ops:
  0.6 11.1 %collective-permute-start = (bf16[1,64,3584]{2,1,0:T(8,128)(2,1)}, bf16[1,64,3584]{2,1,0:T(8,128)(2,1)S(1)}, u32[]{:S(2)}, u32[]{:S(2)}) collective-permute-start(bf16[1,64,3584]{2,1,0:T(8,128)(2,1)} %param.10), channel_id=1, source_target_pairs={{0,48},{48,96},{96,144},{144,192},{192,240},{240,288},{288,336},{3... | collective-permute-start | bytes 1376264 | tf_op jit(solution)/shard_map/ppermute | solution.py:15
  11.7 1.9 %collective-permute-start.1 = (bf16[1,64,3584]{2,1,0:T(8,128)(2,1)}, bf16[1,64,3584]{2,1,0:T(8,128)(2,1)S(1)}, u32[]{:S(2)}, u32[]{:S(2)}) collective-permute-start(bf16[1,64,3584]{2,1,0:T(8,128)(2,1)} %param.12), channel_id=1, source_target_pairs={{0,720},{48,0},{96,48},{144,96},{192,144},{240,192},{288,240},{336... | collective-permute-start | bytes 1376264 | tf_op jit(solution)/shard_map/ppermute | solution.py:15
  13.6 0.8 copy.20
  14.5 0.8 copy.22
  15.3 1.5 %copy.24 = bf16[1,3584,128]{1,2,0:T(8,128)(2,1)S(1)} copy(bf16[1,3584,128]{2,1,0:T(8,128)(2,1)} %param.13) | data formatting | bytes 1835008 | tf_op args[3]
  16.8 1.5 %copy.25 = bf16[1,3584,128]{1,2,0:T(8,128)(2,1)S(1)} copy(bf16[1,3584,128]{2,1,0:T(8,128)(2,1)} %param.14) | data formatting | bytes 1835008 | tf_op args[4]
  18.3 0.2 convolution_convert_fusion.1
  18.6 7.6 %collective-permute-done.1 = bf16[1,64,3584]{2,1,0:T(8,128)(2,1)S(1)} collective-permute-done((bf16[1,64,3584]{2,1,0:T(8,128)(2,1)}, bf16[1,64,3584]{2,1,0:T(8,128)(2,1)S(1)}, u32[]{:S(2)}, u32[]{:S(2)}) %collective-permute-start.1) | collective-permute-done | bytes 458784 | tf_op jit(solution)/shard_map/ppermute | solution.py:15
  26.2 0.2 convolution_convert_fusion
  26.6 1.0 broadcast_in_dim.6
  27.6 15.1 %all-to-all-start = ((bf16[24,4,3584]{2,1,0:T(4,128)(2,1)}), bf16[24,4,3584]{2,1,0:T(4,128)(2,1)S(1)}, u32[]{:S(2)}, u32[]{:S(2)}) async-start(bf16[24,4,3584]{2,1,0:T(4,128)(2,1)} %bitcast.34), calls=%async_computation | async-start | bytes 1376256 | tf_op jit(solution)/shard_map/all_to_all | solution.py:207
  42.7 1.9 %collective-permute-start.2 = (bf16[128,3584]{1,0:T(8,128)(2,1)}, bf16[128,3584]{1,0:T(8,128)(2,1)}, u32[]{:S(2)}, u32[]{:S(2)}) collective-permute-start(bf16[128,3584]{1,0:T(8,128)(2,1)} %bitcast.35), channel_id=1, source_target_pairs={{0,1},{1,0},{2,3},{3,2},{4,5},{5,4},{6,7},{7,6},{8,9},{9,8},{10,11... | collective-permute-start | bytes 2752520 | tf_op jit(solution)/shard_map/ppermute | solution.py:20
  44.7 2.4 %collective-permute-start.3 = (bf16[128,3584]{1,0:T(8,128)(2,1)S(1)}, bf16[128,3584]{1,0:T(8,128)(2,1)}, u32[]{:S(2)}, u32[]{:S(2)}) collective-permute-start(bf16[128,3584]{1,0:T(8,128)(2,1)S(1)} %bitcast.32), channel_id=1, source_target_pairs={{0,1},{1,0},{2,3},{3,2},{4,5},{5,4},{6,7},{7,6},{8,9},{9,8},{10,11... | collective-permute-start | bytes 2752520 | tf_op jit(solution)/shard_map/ppermute | solution.py:20
  47.1 1.9 %collective-permute-start.4 = (bf16[128,3584]{1,0:T(8,128)(2,1)S(1)}, bf16[128,3584]{1,0:T(8,128)(2,1)}, u32[]{:S(2)}, u32[]{:S(2)}) collective-permute-start(bf16[128,3584]{1,0:T(8,128)(2,1)S(1)} %bitcast.30), channel_id=1, source_target_pairs={{0,1},{1,0},{2,3},{3,2},{4,5},{5,4},{6,7},{7,6},{8,9},{9,8},{10,11... | collective-permute-start | bytes 2752520 | tf_op jit(solution)/shard_map/ppermute | solution.py:20
  49.1 2.4 %collective-permute-start.5 = (bf16[24,2,2,128]{3,1,0,2:T(2,128)(2,1)S(1)}, bf16[24,2,2,128]{3,1,0,2:T(2,128)(2,1)S(1)}, u32[]{:S(2)}, u32[]{:S(2)}) collective-permute-start(bf16[24,2,2,128]{3,1,0,2:T(2,128)(2,1)S(1)} %bitcast.41), channel_id=1, source_target_pairs={{0,1},{1,0},{2,3},{3,2},{4,5},{5,4},{6,7},{7,6},{8,9},{9,8},{10,11... | collective-permute-start | bytes 73736 | tf_op jit(solution)/shard_map/ppermute | solution.py:20
  51.6 2.9 %pad_maximum_fusion.own = bf16[384,3584]{1,0:T(8,128)(2,1)} fusion(bf16[128,3584]{1,0:T(8,128)(2,1)S(1)} %bitcast.31, bf16[128,3584]{1,0:T(8,128)(2,1)S(1)} %bitcast.33, bf16[128,3584]{1,0:T(8,128)(2,1)} %bitcast.36), kind=kLoop, calls=%fused_computation.2 | loop fusion | flops 8257536 | bytes 5505024 | tf_op jit(solution)/shard_map/concatenate | solution.py:209
  54.5 0.7 pad_convert_fusion.1
  55.1 0.7 pad_convert_fusion
  55.8 17.9 %all-to-all-done.rows = bf16[24,4,3584]{2,1,0:T(4,128)(2,1)S(1)} async-done(((bf16[24,4,3584]{2,1,0:T(4,128)(2,1)}), bf16[24,4,3584]{2,1,0:T(4,128)(2,1)S(1)}, u32[]{:S(2)}, u32[]{:S(2)}) %all-to-all-start) | async-done | bytes 688160 | tf_op jit(solution)/shard_map/all_to_all | solution.py:207
  73.7 0.9 copy-done
  74.6 7.0 %expert.1 = bf16[24,4,3584]{2,1,0:T(4,128)(2,1)} custom-call(bf16[24,4,3584]{2,1,0:T(4,128)(2,1)} %copy-done, bf16[384,3584]{1,0:T(8,128)(2,1)} %pad_maximum_fusion.own, bf16[128,3584]{1,0:T(8,128)(2,1)} %collective-permute-done.2.other_down, bf16[128,3584]{1,0:T(8,128)(2,1)} %collective-permute-done.3.other_gate, ...), custom_call_target="tpu_custom_call" | custom-call | flops 1056964608 | bytes 5505024 | tf_op jit(solution)/shard_map/expert/pallas_call | solution.py:146
  81.6 5.9 %all-to-all-start.1 = ((bf16[24,4,3584]{2,1,0:T(4,128)(2,1)}), bf16[24,4,3584]{2,1,0:T(4,128)(2,1)S(1)}, u32[]{:S(2)}, u32[]{:S(2)}) async-start(bf16[24,4,3584]{2,1,0:T(4,128)(2,1)} %expert.1), calls=%async_computation.1 | async-start | bytes 1376256 | tf_op jit(solution)/shard_map/all_to_all | solution.py:220
  87.9 29.6 %all-to-all-done.1.back = bf16[24,4,3584]{2,1,0:T(4,128)(2,1)S(1)} async-done(((bf16[24,4,3584]{2,1,0:T(4,128)(2,1)}), bf16[24,4,3584]{2,1,0:T(4,128)(2,1)S(1)}, u32[]{:S(2)}, u32[]{:S(2)}) %all-to-all-start.1) | async-done | bytes 688160 | tf_op jit(solution)/shard_map/all_to_all | solution.py:220
  117.5 1.8 %settle.1 = (bf16[64,3584]{1,0:T(8,128)(2,1)}, bf16[64,3584]{1,0:T(8,128)(2,1)}) custom-call(s32[6]{0:T(128)S(1)} %reshape.37.fwd_slots, f32[6]{0:T(128)S(1)} %reshape.38.fwd_gates, s32[6]{0:T(128)S(1)} %reshape.39.bwd_slots, f32[6]{0:T(128)S(1)} %reshape.40.bwd_gates, bf16[24,4,3584]{2,1,0:T(4,128)(2,1)S(1)} %all-to-all-done.1.back, ...), custom_call_target="tpu_custom_call" | custom-call | flops 688128 | bytes 2293760 | tf_op jit(solution)/shard_map/settle/pallas_call | solution.py:60
  (24 shorter events, 0.8 us)
Async XLA Ops:
  0.6 17.6 %collective-permute-start = (bf16[1,64,3584]{2,1,0:T(8,128)(2,1)}, bf16[1,64,3584]{2,1,0:T(8,128)(2,1)S(1)}, u32[]{:S(2)}, u32[]{:S(2)}) collective-permute-start(bf16[1,64,3584]{2,1,0:T(8,128)(2,1)} %param.10), channel_id=1, source_target_pairs={{0,48},{48,96},{96,144},{144,192},{192,240},{240,288},{288,336},{3... | collective-permute-start | bytes 1376264 | tf_op jit(solution)/shard_map/ppermute | solution.py:15
  11.7 14.5 %collective-permute-start.1 = (bf16[1,64,3584]{2,1,0:T(8,128)(2,1)}, bf16[1,64,3584]{2,1,0:T(8,128)(2,1)S(1)}, u32[]{:S(2)}, u32[]{:S(2)}) collective-permute-start(bf16[1,64,3584]{2,1,0:T(8,128)(2,1)} %param.12), channel_id=1, source_target_pairs={{0,720},{48,0},{96,48},{144,96},{192,144},{240,192},{288,240},{336... | collective-permute-start | bytes 1376264 | tf_op jit(solution)/shard_map/ppermute | solution.py:15
  16.8 32.3 %copy-start.1 = (bf16[1,48,2,2,128]{4,3,2,1,0:T(2,128)(2,1)S(1)}, bf16[1,48,2,2,128]{4,3,2,1,0:T(2,128)(2,1)}, u32[]{:S(2)}) copy-start(bf16[1,48,2,2,128]{4,3,2,1,0:T(2,128)(2,1)} %param.11) | copy-start | bytes 147460
  27.6 46.1 %all-to-all-start = ((bf16[24,4,3584]{2,1,0:T(4,128)(2,1)}), bf16[24,4,3584]{2,1,0:T(4,128)(2,1)S(1)}, u32[]{:S(2)}, u32[]{:S(2)}) async-start(bf16[24,4,3584]{2,1,0:T(4,128)(2,1)} %bitcast.34), calls=%async_computation | async-start | bytes 1376256 | tf_op jit(solution)/shard_map/all_to_all | solution.py:207
  42.7 13.1 %collective-permute-start.2 = (bf16[128,3584]{1,0:T(8,128)(2,1)}, bf16[128,3584]{1,0:T(8,128)(2,1)}, u32[]{:S(2)}, u32[]{:S(2)}) collective-permute-start(bf16[128,3584]{1,0:T(8,128)(2,1)} %bitcast.35), channel_id=1, source_target_pairs={{0,1},{1,0},{2,3},{3,2},{4,5},{5,4},{6,7},{7,6},{8,9},{9,8},{10,11... | collective-permute-start | bytes 2752520 | tf_op jit(solution)/shard_map/ppermute | solution.py:20
  44.7 11.1 %collective-permute-start.3 = (bf16[128,3584]{1,0:T(8,128)(2,1)S(1)}, bf16[128,3584]{1,0:T(8,128)(2,1)}, u32[]{:S(2)}, u32[]{:S(2)}) collective-permute-start(bf16[128,3584]{1,0:T(8,128)(2,1)S(1)} %bitcast.32), channel_id=1, source_target_pairs={{0,1},{1,0},{2,3},{3,2},{4,5},{5,4},{6,7},{7,6},{8,9},{9,8},{10,11... | collective-permute-start | bytes 2752520 | tf_op jit(solution)/shard_map/ppermute | solution.py:20
  47.1 8.7 %collective-permute-start.4 = (bf16[128,3584]{1,0:T(8,128)(2,1)S(1)}, bf16[128,3584]{1,0:T(8,128)(2,1)}, u32[]{:S(2)}, u32[]{:S(2)}) collective-permute-start(bf16[128,3584]{1,0:T(8,128)(2,1)S(1)} %bitcast.30), channel_id=1, source_target_pairs={{0,1},{1,0},{2,3},{3,2},{4,5},{5,4},{6,7},{7,6},{8,9},{9,8},{10,11... | collective-permute-start | bytes 2752520 | tf_op jit(solution)/shard_map/ppermute | solution.py:20
  49.1 6.0 %collective-permute-start.5 = (bf16[24,2,2,128]{3,1,0,2:T(2,128)(2,1)S(1)}, bf16[24,2,2,128]{3,1,0,2:T(2,128)(2,1)S(1)}, u32[]{:S(2)}, u32[]{:S(2)}) collective-permute-start(bf16[24,2,2,128]{3,1,0,2:T(2,128)(2,1)S(1)} %bitcast.41), channel_id=1, source_target_pairs={{0,1},{1,0},{2,3},{3,2},{4,5},{5,4},{6,7},{7,6},{8,9},{9,8},{10,11... | collective-permute-start | bytes 73736 | tf_op jit(solution)/shard_map/ppermute | solution.py:20
  73.7 0.9 copy-start
  74.6 12.9 %copy-start.2 = (f32[1,1,3,2]{2,3,1,0:T(2,128)S(1)}, f32[1,1,3,2]{2,3,1,0:T(2,128)}, u32[]{:S(2)}) copy-start(f32[1,1,3,2]{2,3,1,0:T(2,128)} %param.17) | copy-start | bytes 76
  74.6 13.1 %copy-start.3 = (f32[1,1,3,2]{2,3,1,0:T(2,128)S(1)}, f32[1,1,3,2]{2,3,1,0:T(2,128)}, u32[]{:S(2)}) copy-start(f32[1,1,3,2]{2,3,1,0:T(2,128)} %param.19) | copy-start | bytes 76
  81.6 35.9 %all-to-all-start.1 = ((bf16[24,4,3584]{2,1,0:T(4,128)(2,1)}), bf16[24,4,3584]{2,1,0:T(4,128)(2,1)S(1)}, u32[]{:S(2)}, u32[]{:S(2)}) async-start(bf16[24,4,3584]{2,1,0:T(4,128)(2,1)} %expert.1), calls=%async_computation.1 | async-start | bytes 1376256 | tf_op jit(solution)/shard_map/all_to_all | solution.py:220
